TPU v7x, 32 devices: a whole 2x2x4 slice. The times are simulated.
32 devices in a mesh: section: 2 (over core), expert: 16 (over z, y, x).
Axes of the slice: x: 2, y: 2, z: 4, core: 2. Of those that a mesh axis runs over, the one named last changes fastest.
Arguments:
- inputs: bfloat16 [2, 2, 2048, 512], P('section', None, 'expert'), may hold values from -6 to 6
- cotangent: bfloat16 [2, 2, 2048, 512], P('section', None, 'expert'), may hold values from -6 to 6
- segments: int32 [2, 2, 2048], P('section', None, 'expert'), may hold values from 0 to 63, never falling along the last dimension, each value on 1 to 128 neighbouring positions
- tasks: int32 [2, 2, 2048, 1], P('section', None, 'expert'), may hold values from 0 to 7; in each aligned block of 128 rows (0 to 127, 128 to 255, ..., all dimensions but the last counted through in order) at most 48 rows name the same one
- table: int32 [2, 8, 2], P('section'), may hold values from 0 to 15, as said below
- capacity: int32 [2], P('section'), may hold values from 192 to 256, as said below
- gains: float32 [2, 3, 512], P('section'), may hold values from 0.1 to 1.9
- w_qkv: bfloat16 [2, 512, 1536], P('section'), may hold values from -0.25 to 0.25
- w_out: bfloat16 [2, 512, 512], P('section'), may hold values from -0.75 to 0.75
- w_cross: bfloat16 [2, 512, 1024], P('section')
- w_router: bfloat16 [2, 512, 16], P('section'), may hold values from -0.1875 to 0.1875
- w_up: bfloat16 [2, 16, 512, 2048], P('section', 'expert'), may hold values from -0.25 to 0.25
- w_down: bfloat16 [2, 16, 2048, 512], P('section', 'expert'), may hold values from -0.125 to 0.125
Outputs:
- layer_out: bfloat16 [2, 2, 2048, 512], P('section', None, 'expert')
- inputs_grad: float32 [2, 2, 2048, 512], P('section', None, 'expert')
- gains_grad: float32 [2, 3, 512], P('section')
- w_qkv_grad: float32 [2, 512, 1536], P('section')
- w_out_grad: float32 [2, 512, 512], P('section')
- w_cross_grad: float32 [2, 512, 1024], P('section')
- w_router_grad: float32 [2, 512, 16], P('section')
- w_up_grad: float32 [2, 16, 512, 2048], P('section', 'expert')
- w_down_grad: float32 [2, 16, 2048, 512], P('section', 'expert')
Inputs may be any that keep to these rules, and one draw needn't show every extreme that they name: `tasks`: in each device's rows of one micro-batch (aligned blocks of 128 tokens) no task occurs more than 48 times, and some task occurs exactly that often. `table`: for each layer every expert belongs to exactly one task, and a task's two experts differ. One of the two layers has capacity 256.
All inputs are finite; a program needn't handle non-finite values.
Results may differ from a plain program's by a relative error of at most 0.015.
Values may be sent and summed in bfloat16 or wider, within the bound.
A program may use at most 192 MiB of HBM per device.

v0:
```python
import jax
import jax.numpy as jnp
from jax import lax
from jax.sharding import PartitionSpec as P

HEADS = 8


EPSILON = 1e-06


def passed_along(value, axis, steps):
    count = lax.axis_size(axis)
    first, last = (max(0, -steps), min(count, count - steps))
    return lax.ppermute(value, axis, [(source, source + steps) for source in range(first, last)])


def rms_norm(value, gain):
    return value * lax.rsqrt(jnp.mean(value * value, axis=-1, keepdims=True) + EPSILON) * gain


def split_heads(block):
    return block.reshape(block.shape[0], HEADS, block.shape[1] // HEADS)


def contract_rows(left, right):
    return lax.dot_general(
        left, right, (((0,), (0,)), ((), ())), preferred_element_type=jnp.float32
    )


def contract_cols(left, right):
    return lax.dot_general(
        left, right, (((1,), (1,)), ((), ())), preferred_element_type=jnp.float32
    )


def send_bound(tok_rows, expert_count):
    return max(2, 6 * tok_rows // expert_count)


def score_block(queries, key_heads, allowed):
    score_scale = queries.shape[-1] ** (-0.5)
    scores = (
        jnp.einsum("qhd,khd->hqk", queries, key_heads, preferred_element_type=jnp.float32)
        * score_scale
    )
    return (jnp.where(allowed[None], scores, -1000000000.0), score_scale)


def attend(queries, key_heads, value_heads, allowed):
    scores, score_scale = score_block(queries, key_heads, allowed)
    top_score = jnp.max(scores, axis=-1, keepdims=True)
    exp_scores = jnp.exp(scores - top_score)
    row_total = jnp.sum(exp_scores, axis=-1, keepdims=True)
    attn_probs = (exp_scores / row_total).astype(jnp.bfloat16)
    mixed_rows = jnp.einsum(
        "hqk,khd->qhd", attn_probs, value_heads, preferred_element_type=jnp.float32
    )
    return (mixed_rows, top_score + jnp.log(row_total))


def attend_back(queries, key_heads, value_heads, allowed, log_total, grad_mixed):
    scores, score_scale = score_block(queries, key_heads, allowed)
    attn_probs = jnp.exp(scores - log_total)
    grad_probs = jnp.einsum(
        "qhd,khd->hqk", grad_mixed, value_heads, preferred_element_type=jnp.float32
    )
    inner_sum = jnp.sum(attn_probs * grad_probs, axis=-1, keepdims=True)
    grad_scores = (attn_probs * (grad_probs - inner_sum)).astype(jnp.bfloat16)
    grad_queries = (
        jnp.einsum("hqk,khd->qhd", grad_scores, key_heads, preferred_element_type=jnp.float32)
        * score_scale
    )
    grad_keys = (
        jnp.einsum("hqk,qhd->khd", grad_scores, queries, preferred_element_type=jnp.float32)
        * score_scale
    )
    grad_values = jnp.einsum(
        "hqk,qhd->khd",
        attn_probs.astype(jnp.bfloat16),
        grad_mixed,
        preferred_element_type=jnp.float32,
    )
    return (grad_queries, grad_keys, grad_values)


def gate_softmax(chosen):
    return jax.nn.softmax(chosen, axis=-1)


def task_experts(task_now, table_now):
    task_hits = (
        task_now[:, None] == jnp.arange(table_now.shape[0], dtype=jnp.int32)[None, :]
    ).astype(jnp.int32)
    return jnp.sum(task_hits[:, :, None] * table_now[None, :, :], axis=1)


def compact_layout(got_counts, cap_now, send_rows, slot_count):
    source_count = got_counts.shape[0]
    end_rows = jnp.cumsum(got_counts)
    starts = end_rows - got_counts
    live_limit = jnp.minimum(end_rows[-1], cap_now)
    slot_ids = jnp.arange(slot_count, dtype=jnp.int32)
    owner_rank = jnp.sum((end_rows[None, :] <= slot_ids[:, None]).astype(jnp.int32), axis=1)
    owner_rank = jnp.minimum(owner_rank, source_count - 1)
    owner_hits = owner_rank[:, None] == jnp.arange(source_count, dtype=jnp.int32)[None, :]
    owner_start = jnp.sum(jnp.where(owner_hits, starts[None, :], 0), axis=1)
    offset = jnp.clip(slot_ids - owner_start, 0, send_rows - 1)
    source = owner_rank * send_rows + offset
    slot_live = slot_ids < live_limit
    row_ids = jnp.arange(send_rows, dtype=jnp.int32)
    row_slot = starts[:, None] + row_ids[None, :]
    row_live = (row_ids[None, :] < got_counts[:, None]) & (row_slot < cap_now)
    row_slot = jnp.clip(row_slot, 0, slot_count - 1).reshape(-1)
    return (source, slot_live, row_slot, row_live.reshape(-1))


def expert_hidden(taken_rows, w_up):
    hidden = jnp.dot(taken_rows, w_up, preferred_element_type=jnp.float32)
    return (hidden, jax.nn.gelu(hidden).astype(jnp.bfloat16))


def layer_forward(
    inputs_now,
    seg_now,
    task_now,
    table_now,
    cap_now,
    gains_now,
    w_qkv,
    w_out,
    w_cross,
    w_router,
    w_up,
    w_down,
    memory_in,
    is_dec,
):
    tok_rows, model_width = inputs_now.shape
    expert_count = lax.axis_size("expert")
    send_rows = send_bound(tok_rows, expert_count)
    slot_count = 2 * tok_rows
    inputs_f32 = inputs_now.astype(jnp.float32)
    normed_a = rms_norm(inputs_f32, gains_now[0]).astype(jnp.bfloat16)
    qkv_rows = jnp.dot(normed_a, w_qkv, preferred_element_type=jnp.float32).astype(jnp.bfloat16)
    positions = jnp.arange(tok_rows, dtype=jnp.int32)
    allowed = (seg_now[:, None] == seg_now[None, :]) & (
        jnp.logical_not(is_dec) | (positions[None, :] <= positions[:, None])
    )
    mixed_rows, log_self = attend(
        split_heads(qkv_rows[:, :model_width]),
        split_heads(qkv_rows[:, model_width : 2 * model_width]),
        split_heads(qkv_rows[:, 2 * model_width :]),
        allowed,
    )
    attn_rows = mixed_rows.reshape(tok_rows, model_width).astype(jnp.bfloat16)
    after_self = inputs_f32 + jnp.dot(attn_rows, w_out, preferred_element_type=jnp.float32)

    def with_cross(residual):
        normed_c = rms_norm(residual, gains_now[1]).astype(jnp.bfloat16)
        cross_q = jnp.dot(
            normed_c, w_cross[:, :model_width], preferred_element_type=jnp.float32
        ).astype(jnp.bfloat16)
        all_keys = jnp.ones((tok_rows, tok_rows), jnp.bool_)
        cross_mixed, log_cross = attend(
            split_heads(cross_q),
            split_heads(memory_in[:, :model_width]),
            split_heads(memory_in[:, model_width:]),
            all_keys,
        )
        cross_rows = cross_mixed.reshape(tok_rows, model_width).astype(jnp.bfloat16)
        return (
            residual + contract_cols(cross_rows, w_cross[:, model_width:]),
            normed_c,
            cross_q,
            cross_rows,
            log_cross,
        )

    def without_cross(residual):
        blank_rows = jnp.zeros((tok_rows, model_width), jnp.bfloat16)
        return (
            residual,
            blank_rows,
            blank_rows,
            blank_rows,
            jnp.zeros((HEADS, tok_rows, 1), jnp.float32),
        )

    after_cross, normed_c, cross_q, cross_rows, log_cross = lax.cond(
        is_dec, with_cross, without_cross, after_self
    )
    normed_m = rms_norm(after_cross, gains_now[2]).astype(jnp.bfloat16)
    expert_pick = task_experts(task_now, table_now)
    logits = jnp.dot(normed_m, w_router, preferred_element_type=jnp.float32)
    chosen = jnp.take_along_axis(logits, expert_pick, axis=1)
    gate_now = gate_softmax(chosen)
    flat_pick = expert_pick.reshape(-1)
    onehot = (flat_pick[:, None] == jnp.arange(expert_count, dtype=jnp.int32)[None, :]).astype(
        jnp.int32
    )
    pair_rank = jnp.sum((jnp.cumsum(onehot, axis=0) - onehot) * onehot, axis=1)
    counts = jnp.sum(onehot, axis=0)
    send_place = flat_pick * send_rows + pair_rank
    pair_rows = jnp.broadcast_to(normed_m[:, None, :], (tok_rows, 2, model_width)).reshape(
        slot_count, model_width
    )
    outgoing = (
        jnp.zeros((expert_count * send_rows, model_width), jnp.bfloat16)
        .at[send_place]
        .set(pair_rows)
    )
    arrived, arrived_counts = (
        lax.all_to_all(
            outgoing.reshape(expert_count, send_rows, model_width),
            "expert",
            split_axis=0,
            concat_axis=0,
            tiled=True,
        ),
        lax.all_to_all(
            counts.reshape(expert_count, 1), "expert", split_axis=0, concat_axis=0, tiled=True
        ),
    )
    source, slot_live, row_slot, row_live = compact_layout(
        arrived_counts[:, 0], cap_now, send_rows, slot_count
    )
    taken_rows = jnp.where(slot_live[:, None], arrived.reshape(-1, model_width)[source], 0)
    hidden, act_rows = expert_hidden(taken_rows, w_up)
    result = jnp.dot(act_rows, w_down, preferred_element_type=jnp.float32).astype(jnp.bfloat16)
    reply_rows = jnp.where(row_live[:, None], result[row_slot], 0)
    returned = lax.all_to_all(
        reply_rows.reshape(expert_count, send_rows, model_width),
        "expert",
        split_axis=0,
        concat_axis=0,
        tiled=True,
    )
    pair_out = (
        returned.reshape(-1, model_width)[send_place]
        .astype(jnp.float32)
        .reshape(tok_rows, 2, model_width)
    )
    layer_final = after_cross + jnp.sum(gate_now[:, :, None] * pair_out, axis=1)

    def make_memory(residual):
        normed_k = rms_norm(residual, gains_now[1]).astype(jnp.bfloat16)
        return (
            jnp.dot(normed_k, w_cross, preferred_element_type=jnp.float32).astype(jnp.bfloat16),
            normed_k,
        )

    def skip_memory(residual):
        return (
            jnp.zeros((tok_rows, 2 * model_width), jnp.bfloat16),
            jnp.zeros((tok_rows, model_width), jnp.bfloat16),
        )

    memory_out, normed_k = lax.cond(is_dec, skip_memory, make_memory, layer_final)
    saved = {
        "inputs_f32": inputs_f32,
        "normed_a": normed_a,
        "qkv_rows": qkv_rows,
        "allowed": allowed,
        "log_self": log_self,
        "attn_rows": attn_rows,
        "after_self": after_self,
        "normed_c": normed_c,
        "cross_q": cross_q,
        "cross_rows": cross_rows,
        "log_cross": log_cross,
        "memory_in": memory_in,
        "after_cross": after_cross,
        "normed_m": normed_m,
        "expert_pick": expert_pick,
        "gate_now": gate_now,
        "chosen": chosen,
        "send_place": send_place,
        "source": source,
        "slot_live": slot_live,
        "row_slot": row_slot,
        "row_live": row_live,
        "taken_rows": taken_rows,
        "pair_out": pair_out,
        "layer_final": layer_final,
        "normed_k": normed_k,
    }
    saved["hidden"] = hidden
    saved["act_rows"] = act_rows
    return (layer_final, memory_out, saved)


def layer_backward(
    saved, grad_final, grad_memory, gains_now, w_qkv, w_out, w_cross, w_router, w_up, w_down, is_dec
):
    tok_rows, model_width = grad_final.shape
    expert_count = lax.axis_size("expert")
    send_rows = send_bound(tok_rows, expert_count)

    def memory_back(grad_pack):
        grad_top, grad_mem = grad_pack
        grad_normed = contract_cols(grad_mem, w_cross)
        grad_weight = contract_rows(saved["normed_k"], grad_mem)
        norm_out, pull_norm = jax.vjp(rms_norm, saved["layer_final"], gains_now[1])
        grad_state, grad_gain = pull_norm(grad_normed)
        return (grad_top + grad_state, grad_weight, grad_gain)

    def memory_skip(grad_pack):
        return (
            grad_pack[0],
            jnp.zeros((model_width, 2 * model_width), jnp.float32),
            jnp.zeros((model_width,), jnp.float32),
        )

    grad_final, grad_cross_mem, grad_gain_mem = lax.cond(
        is_dec, memory_skip, memory_back, (grad_final, grad_memory)
    )
    gate_now = saved["gate_now"]
    pair_out = saved["pair_out"]
    grad_pair = (
        (gate_now[:, :, None] * grad_final[:, None, :])
        .astype(jnp.bfloat16)
        .reshape(-1, model_width)
    )
    grad_gates = jnp.sum(pair_out * grad_final[:, None, :], axis=-1)
    expert_pick = saved["expert_pick"]
    gate_out, pull_gate = jax.vjp(gate_softmax, saved["chosen"])
    grad_chosen = pull_gate(grad_gates)[0]
    expert_ids = jnp.arange(w_router.shape[1], dtype=jnp.int32)
    grad_logits = jnp.sum(
        jnp.where(
            expert_pick[:, :, None] == expert_ids[None, None, :], grad_chosen[:, :, None], 0.0
        ),
        axis=1,
    )
    grad_normed_route = lax.dot_general(
        grad_logits,
        w_router.astype(jnp.float32),
        (((1,), (1,)), ((), ())),
        precision=lax.Precision.HIGHEST,
        preferred_element_type=jnp.float32,
    )
    grad_router = lax.dot_general(
        saved["normed_m"].astype(jnp.float32),
        grad_logits,
        (((0,), (0,)), ((), ())),
        precision=lax.Precision.HIGHEST,
        preferred_element_type=jnp.float32,
    )
    outgoing = (
        jnp.zeros((expert_count * send_rows, model_width), jnp.bfloat16)
        .at[saved["send_place"]]
        .set(grad_pair)
    )
    arrived_grad = lax.all_to_all(
        outgoing.reshape(expert_count, send_rows, model_width),
        "expert",
        split_axis=0,
        concat_axis=0,
        tiled=True,
    )
    grad_result = jnp.where(
        saved["slot_live"][:, None], arrived_grad.reshape(-1, model_width)[saved["source"]], 0
    )
    hidden = saved["hidden"]
    act_rows = saved["act_rows"]
    grad_act = contract_cols(grad_result, w_down)
    grad_down = contract_rows(act_rows, grad_result)
    gelu_out, pull_gelu = jax.vjp(jax.nn.gelu, hidden)
    grad_hidden = pull_gelu(grad_act)[0].astype(jnp.bfloat16)
    grad_up = contract_rows(saved["taken_rows"], grad_hidden)
    grad_taken = contract_cols(grad_hidden, w_up).astype(jnp.bfloat16)
    reply_rows = jnp.where(saved["row_live"][:, None], grad_taken[saved["row_slot"]], 0)
    returned = lax.all_to_all(
        reply_rows.reshape(expert_count, send_rows, model_width),
        "expert",
        split_axis=0,
        concat_axis=0,
        tiled=True,
    )
    grad_pairs = returned.reshape(-1, model_width)[saved["send_place"]].astype(jnp.float32)
    grad_pairs = grad_pairs.reshape(tok_rows, 2, model_width)
    grad_normed_m = grad_normed_route + grad_pairs[:, 0] + grad_pairs[:, 1]
    norm_out, pull_norm = jax.vjp(rms_norm, saved["after_cross"], gains_now[2])
    grad_state, grad_gain_moe = pull_norm(grad_normed_m)
    grad_after_cross = grad_final + grad_state

    def cross_back(grad_top):
        grad_y = grad_top.astype(jnp.bfloat16)
        grad_wo = contract_rows(grad_y, saved["cross_rows"])
        grad_mix = jnp.dot(
            grad_y, w_cross[:, model_width:], preferred_element_type=jnp.float32
        ).astype(jnp.bfloat16)
        memory_in = saved["memory_in"]
        all_keys = jnp.ones((tok_rows, tok_rows), jnp.bool_)
        grad_q, grad_k, grad_v = attend_back(
            split_heads(saved["cross_q"]),
            split_heads(memory_in[:, :model_width]),
            split_heads(memory_in[:, model_width:]),
            all_keys,
            saved["log_cross"],
            split_heads(grad_mix),
        )
        grad_q = grad_q.reshape(tok_rows, model_width).astype(jnp.bfloat16)
        grad_wq = contract_rows(saved["normed_c"], grad_q)
        grad_nc = contract_cols(grad_q, w_cross[:, :model_width])
        norm_out_c, pull_cross = jax.vjp(rms_norm, saved["after_self"], gains_now[1])
        grad_state_c, grad_gain_c = pull_cross(grad_nc)
        grad_mem = jnp.concatenate(
            [grad_k.reshape(tok_rows, model_width), grad_v.reshape(tok_rows, model_width)], axis=1
        ).astype(jnp.bfloat16)
        return (
            grad_top + grad_state_c,
            jnp.concatenate([grad_wq, grad_wo], axis=1),
            grad_gain_c,
            grad_mem,
        )

    def cross_skip(grad_top):
        return (
            grad_top,
            jnp.zeros((model_width, 2 * model_width), jnp.float32),
            jnp.zeros((model_width,), jnp.float32),
            jnp.zeros((tok_rows, 2 * model_width), jnp.bfloat16),
        )

    grad_after_self, grad_cross_dec, grad_gain_dec, grad_mem_out = lax.cond(
        is_dec, cross_back, cross_skip, grad_after_cross
    )
    grad_y = grad_after_self.astype(jnp.bfloat16)
    grad_wout = contract_rows(saved["attn_rows"], grad_y)
    grad_mix = contract_cols(grad_y, w_out).astype(jnp.bfloat16)
    qkv_rows = saved["qkv_rows"]
    grad_q, grad_k, grad_v = attend_back(
        split_heads(qkv_rows[:, :model_width]),
        split_heads(qkv_rows[:, model_width : 2 * model_width]),
        split_heads(qkv_rows[:, 2 * model_width :]),
        saved["allowed"],
        saved["log_self"],
        split_heads(grad_mix),
    )
    grad_qkv = jnp.concatenate(
        [
            grad_q.reshape(tok_rows, model_width),
            grad_k.reshape(tok_rows, model_width),
            grad_v.reshape(tok_rows, model_width),
        ],
        axis=1,
    ).astype(jnp.bfloat16)
    grad_wqkv = contract_rows(saved["normed_a"], grad_qkv)
    grad_na = contract_cols(grad_qkv, w_qkv)
    norm_out_a, pull_self = jax.vjp(rms_norm, saved["inputs_f32"], gains_now[0])
    grad_state_a, grad_gain_self = pull_self(grad_na)
    grad_inputs = grad_after_self + grad_state_a
    grad_gains = jnp.stack([grad_gain_self, grad_gain_mem + grad_gain_dec, grad_gain_moe])
    dense = (grad_gains, grad_wqkv, grad_wout, grad_cross_mem + grad_cross_dec, grad_router)
    return (grad_inputs, dense, grad_up, grad_down, grad_mem_out)


def shards(
    inputs,
    cotangent,
    segments,
    tasks,
    table,
    capacity,
    gains,
    w_qkv,
    w_out,
    w_cross,
    w_router,
    w_up,
    w_down,
):
    section_index = lax.axis_index("section")
    is_dec = section_index == 1
    micro_count = inputs.shape[1]
    tok_rows = inputs.shape[2]
    model_width = inputs.shape[3]
    gains_now = gains[0]
    weights_now = (w_qkv[0], w_out[0], w_cross[0], w_router[0], w_up[0, 0], w_down[0, 0])
    memory_state = jnp.zeros((tok_rows, 2 * model_width), jnp.bfloat16)
    layer_rows = jnp.zeros((micro_count, tok_rows, model_width), jnp.bfloat16)
    saved_ticks = []
    for moment in range(micro_count + 1):
        micro_index = moment - section_index
        is_live = (micro_index >= 0) & (micro_index < micro_count)
        micro_pick = jnp.clip(micro_index, 0, micro_count - 1)
        if moment == 0:
            memory_in = memory_state
        else:
            memory_in = passed_along(memory_state, "section", 1)
        inputs_now = lax.dynamic_index_in_dim(inputs[0], micro_pick, 0, keepdims=False)
        seg_now = lax.dynamic_index_in_dim(segments[0], micro_pick, 0, keepdims=False)
        task_now = lax.dynamic_index_in_dim(tasks[0], micro_pick, 0, keepdims=False)[:, 0]
        layer_final, memory_state, saved = layer_forward(
            inputs_now,
            seg_now,
            task_now,
            table[0],
            capacity[0],
            gains_now,
            weights_now[0],
            weights_now[1],
            weights_now[2],
            weights_now[3],
            weights_now[4],
            weights_now[5],
            memory_in,
            is_dec,
        )
        updated = lax.dynamic_update_index_in_dim(
            layer_rows, layer_final.astype(jnp.bfloat16), micro_pick, 0
        )
        layer_rows = jnp.where(is_live, updated, layer_rows)
        saved_ticks.append(saved)
    dense_total = (
        jnp.zeros((3, model_width), jnp.float32),
        jnp.zeros(w_qkv.shape[1:], jnp.float32),
        jnp.zeros(w_out.shape[1:], jnp.float32),
        jnp.zeros(w_cross.shape[1:], jnp.float32),
        jnp.zeros(w_router.shape[1:], jnp.float32),
    )
    up_total = jnp.zeros(w_up.shape[2:], jnp.float32)
    down_total = jnp.zeros(w_down.shape[2:], jnp.float32)
    grad_rows = jnp.zeros((micro_count, tok_rows, model_width), jnp.float32)
    grad_memory = jnp.zeros((tok_rows, 2 * model_width), jnp.bfloat16)
    for backward_step in range(micro_count + 1):
        moment = micro_count - backward_step
        micro_index = moment - section_index
        is_live = (micro_index >= 0) & (micro_index < micro_count)
        micro_pick = jnp.clip(micro_index, 0, micro_count - 1)
        if backward_step == 0:
            grad_from_dec = grad_memory
        else:
            grad_from_dec = passed_along(grad_memory, "section", -1)
        grad_from_dec = jnp.where(is_live, grad_from_dec, jnp.zeros_like(grad_from_dec))
        cot_now = lax.dynamic_index_in_dim(cotangent[0], micro_pick, 0, keepdims=False).astype(
            jnp.float32
        )
        grad_final = jnp.where(is_live, cot_now, 0.0)
        grad_inputs, dense, grad_up, grad_down, grad_memory = layer_backward(
            saved_ticks[moment],
            grad_final,
            grad_from_dec,
            gains_now,
            weights_now[0],
            weights_now[1],
            weights_now[2],
            weights_now[3],
            weights_now[4],
            weights_now[5],
            is_dec,
        )
        updated = lax.dynamic_update_index_in_dim(grad_rows, grad_inputs, micro_pick, 0)
        grad_rows = jnp.where(is_live, updated, grad_rows)
        up_total = up_total + grad_up
        down_total = down_total + grad_down
        dense_total = tuple((total + piece for total, piece in zip(dense_total, dense)))
    dense_total = lax.psum(
        (dense_total[0], dense_total[1], dense_total[2], dense_total[3], dense_total[4]), "expert"
    )
    return (
        layer_rows[None],
        grad_rows[None],
        dense_total[0][None],
        dense_total[1][None],
        dense_total[2][None],
        dense_total[3][None],
        dense_total[4][None],
        up_total[None, None],
        down_total[None, None],
    )


def solution(mesh):
    in_specs = (
        P("section", None, "expert", None),
        P("section", None, "expert", None),
        P("section", None, "expert"),
        P("section", None, "expert", None),
        P("section", None, None),
        P("section"),
        P("section", None, None),
        P("section", None, None),
        P("section", None, None),
        P("section", None, None),
        P("section", None, None),
        P("section", "expert", None, None),
        P("section", "expert", None, None),
    )
    out_specs = (
        P("section", None, "expert", None),
        P("section", None, "expert", None),
        P("section", None, None),
        P("section", None, None),
        P("section", None, None),
        P("section", None, None),
        P("section", None, None),
        P("section", "expert", None, None),
        P("section", "expert", None, None),
    )
    return jax.shard_map(shards, mesh=mesh, in_specs=in_specs, out_specs=out_specs, check_vma=False)
```

profile of v0, /device:TPU:0, one launch (start us, length us, event | category | flops | bytes accessed | tf_op | source)
XLA Modules:
  0.0 884.2 jit_solution(10892725822737657713)
XLA Ops:
  11.5 8.4 all-to-all-start
  55.2 6.9 all-to-all-start.1
  82.2 7.1 all-to-all-start.3
  103.0 7.0 all-to-all-start.2
  115.9 10.8 %all-to-all-done.2 = bf16[16,48,512]{2,1,0:T(8,128)(2,1)} async-done(((bf16[16,48,512]{2,1,0:T(8,128)(2,1)}), bf16[16,48,512]{2,1,0:T(8,128)(2,1)}, u32[]{:S(2)}, u32[]{:S(2)}) %all-to-all-start.2) | async-done | bytes 786464 | tf_op jit(solution)/shard_map/all_to_all | solution.py:233
  126.6 8.8 all-to-all-start.6
  144.9 4.7 conditional.13
  166.1 7.3 all-to-all-start.4
  202.1 9.4 %all-to-all-start.5 = ((bf16[16,48,512]{2,1,0:T(8,128)(2,1)}), bf16[16,48,512]{2,1,0:T(8,128)(2,1)}, u32[]{:S(2)}, u32[]{:S(2)}) async-start(bf16[16,48,512]{2,1,0:T(8,128)(2,1)} %broadcast_select_fusion.9), calls=%async_computation.5 | async-start | bytes 1572864 | tf_op jit(solution)/shard_map/all_to_all | solution.py:233
  219.4 11.7 %all-to-all-done.5 = bf16[16,48,512]{2,1,0:T(8,128)(2,1)} async-done(((bf16[16,48,512]{2,1,0:T(8,128)(2,1)}), bf16[16,48,512]{2,1,0:T(8,128)(2,1)}, u32[]{:S(2)}, u32[]{:S(2)}) %all-to-all-start.5) | async-done | bytes 786464 | tf_op jit(solution)/shard_map/all_to_all | solution.py:233
  238.4 5.4 conditional.15
  260.6 7.2 all-to-all-start.7
  272.9 10.2 %all-to-all-done.7 = bf16[16,48,512]{2,1,0:T(8,128)(2,1)} async-done(((bf16[16,48,512]{2,1,0:T(8,128)(2,1)}), bf16[16,48,512]{2,1,0:T(8,128)(2,1)}, u32[]{:S(2)}, u32[]{:S(2)}) %all-to-all-start.7) | async-done | bytes 786464 | tf_op jit(solution)/shard_map/all_to_all | solution.py:215
  296.6 9.0 %all-to-all-start.8 = ((bf16[16,48,512]{2,1,0:T(8,128)(2,1)}), bf16[16,48,512]{2,1,0:T(8,128)(2,1)}, u32[]{:S(2)}, u32[]{:S(2)}) async-start(bf16[16,48,512]{2,1,0:T(8,128)(2,1)} %broadcast_select_fusion.7), calls=%async_computation.8 | async-start | bytes 1572864 | tf_op jit(solution)/shard_map/all_to_all | solution.py:233
  315.4 9.5 %all-to-all-done.8 = bf16[16,48,512]{2,1,0:T(8,128)(2,1)} async-done(((bf16[16,48,512]{2,1,0:T(8,128)(2,1)}), bf16[16,48,512]{2,1,0:T(8,128)(2,1)}, u32[]{:S(2)}, u32[]{:S(2)}) %all-to-all-start.8) | async-done | bytes 786464 | tf_op jit(solution)/shard_map/all_to_all | solution.py:233
  334.4 6.0 conditional.18
  347.5 24.5 %all_to_all.96 = bf16[16,48,512]{2,1,0:T(8,128)(2,1)} all-to-all(bf16[16,48,512]{2,1,0:T(8,128)(2,1)} %bitcast.682), channel_id=1, replica_groups=mesh['section'=2,'expert'=16] {'expert'}, dimensions={0} | all-to-all | bytes 1572864 | tf_op jit(solution)/shard_map/all_to_all | solution.py:356
  386.1 4.3 all-to-all-start.10
  396.5 11.2 %all-to-all-done.10 = bf16[16,48,512]{2,1,0:T(8,128)(2,1)} async-done(((bf16[16,48,512]{2,1,0:T(8,128)(2,1)}), bf16[16,48,512]{2,1,0:T(8,128)(2,1)}, u32[]{:S(2)}, u32[]{:S(2)}) %all-to-all-start.10) | async-done | bytes 786464 | tf_op jit(solution)/shard_map/all_to_all | solution.py:375
  426.1 11.3 %collective-permute-done.2 = bf16[128,1024]{1,0:T(8,128)(2,1)} collective-permute-done((bf16[128,1024]{1,0:T(8,128)(2,1)S(1)}, bf16[128,1024]{1,0:T(8,128)(2,1)}, u32[]{:S(2)}, u32[]{:S(2)}) %collective-permute-start.2) | collective-permute-done | bytes 262176 | tf_op jit(solution)/shard_map/ppermute | solution.py:15
  437.4 11.3 %conditional.20 = (f32[128,512]{1,0:T(8,128)}, f32[512]{0:T(512)}, f32[512,1024]{1,0:T(8,128)}) conditional(s32[]{:T(128)} %convert_element_type.489, (pred[]{:T(512)}, bf16[128,1024]{1,0:T(8,128)(2,1)}, bf16[128,1024]{1,0:T(8,128)(2,1)}, bf16[512,1024]{1,0:T(8,128)(2,1)S(1)}, f32[3,512]{1,0:T(4,128)}, /*index=5*/f32[128,512]{1,0:T(8,128)}, ...), branch_computations={%region_90.95_spmd, %region_94.96_spmd} | conditional | flops 269615360 | bytes 12467282 | solution.py:316
  455.9 9.3 %all-to-all-start.11 = ((bf16[16,48,512]{2,1,0:T(8,128)(2,1)}), bf16[16,48,512]{2,1,0:T(8,128)(2,1)}, u32[]{:S(2)}, u32[]{:S(2)}) async-start(bf16[16,48,512]{2,1,0:T(8,128)(2,1)} %bitcast.680), calls=%async_computation.11 | async-start | bytes 1572864 | tf_op jit(solution)/shard_map/all_to_all | solution.py:356
  473.6 4.9 all-to-all-done.11
  492.7 4.6 all-to-all-start.12
  531.8 6.8 collective-permute-done.3
  538.7 10.7 %conditional.22 = (f32[128,512]{1,0:T(8,128)S(1)}, f32[512]{0:T(512)}, f32[512,1024]{1,0:T(8,128)}) conditional(s32[]{:T(128)} %convert_element_type.489, (pred[]{:T(512)}, bf16[128,1024]{1,0:T(8,128)(2,1)S(1)}, bf16[128,1024]{1,0:T(8,128)(2,1)}, bf16[512,1024]{1,0:T(8,128)(2,1)S(1)}, f32[3,512]{1,0:T(4,128)}, ...), branch_computations={%region_108.113_spmd, %region_112.114_spmd} | conditional | flops 269615360 | bytes 10370074 | solution.py:316
  555.6 5.1 all-to-all-start.13
  589.1 4.6 all-to-all-start.14
  597.8 4.3 convolution_add_fusion.4
  634.0 6.5 add_bitcast_fusion.5
  660.8 78.7 %all-reduce = (f32[1,3,512]{2,0,1:T(1,128)}, f32[1,512,16]{1,2,0:T(8,128)}) all-reduce(f32[1,3,512]{2,0,1:T(1,128)S(1)} %broadcast_in_dim.504, f32[1,512,16]{1,2,0:T(8,128)S(1)} %fusion.159), channel_id=1, replica_groups=mesh['section'=2,'expert'=16] {'expert'}, use_global_device_ids=true, to_apply=%region_132.134 | all-reduce | flops 9728 | bytes 77824 | tf_op jit(solution)/shard_map/psum | solution.py:561
  740.7 129.1 %all-reduce.4.cloned.1.call-done = (f32[1,512,1536]{2,1,0:T(8,128)}, f32[1,512,512]{2,1,0:T(8,128)}, f32[1,512,1024]{2,1,0:T(8,128)}) async-done(((f32[1,512,1536]{2,1,0:T(8,128)}, f32[1,512,512]{2,1,0:T(8,128)}, f32[1,512,1024]{2,1,0:T(8,128)}), (f32[1,512,1536]{2,1,0:T(8,128)}, f32[1,512,512]{2,1,0:T(8,128)}, f32[1,512,1024]{2,1,0:T(8,128)})) %all-reduce.4.cloned.1.call-update) | async-done | bytes 6291472 | tf_op jit(solution)/shard_map/psum | solution.py:561
  (832 shorter events, 464.6 us)
Async XLA Ops:
  7.2 89.3 %copy-start = (bf16[1,1,2048,512]{3,2,1,0:T(8,128)(2,1)S(1)}, bf16[1,1,2048,512]{3,2,1,0:T(8,128)(2,1)}, u32[]{:S(2)}) copy-start(bf16[1,1,2048,512]{3,2,1,0:T(8,128)(2,1)} %param.51) | copy-start | bytes 6291460
  8.9 23.2 %copy-start.130 = (s32[128,2]{0,1:T(2,128)}, s32[128,2]{0,1:T(2,128)S(1)}, u32[]{:S(2)}) copy-start(s32[128,2]{0,1:T(2,128)S(1)} %get-tuple-element.591) | copy-start | bytes 3076
  9.1 26.1 %copy-start.10 = (bf16[1,2,128,512]{3,2,1,0:T(8,128)(2,1)S(1)}, bf16[1,2,128,512]{3,2,1,0:T(8,128)(2,1)}, u32[]{:S(2)}) copy-start(bf16[1,2,128,512]{3,2,1,0:T(8,128)(2,1)} %param.39) | copy-start | bytes 786436
  11.5 38.6 %all-to-all-start = ((s32[16,1,1]{2,1,0:T(1,128)}), s32[16,1,1]{2,1,0:T(1,128)}, u32[]{:S(2)}, u32[]{:S(2)}) async-start(s32[16,1,1]{2,1,0:T(1,128)} %copy.438), calls=%async_computation | async-start | bytes 16384 | tf_op jit(solution)/shard_map/all_to_all | solution.py:222
  52.3 22.4 %copy-start.102 = (bf16[128,512]{1,0:T(8,128)(2,1)S(1)}, bf16[128,512]{1,0:T(8,128)(2,1)}, u32[]{:S(2)}) copy-start(bf16[128,512]{1,0:T(8,128)(2,1)} %get-tuple-element.647) | copy-start | bytes 393220
  55.2 27.1 %all-to-all-start.1 = ((bf16[16,48,512]{2,1,0:T(8,128)(2,1)}), bf16[16,48,512]{2,1,0:T(8,128)(2,1)}, u32[]{:S(2)}, u32[]{:S(2)}) async-start(bf16[16,48,512]{2,1,0:T(8,128)(2,1)} %bitcast.677), calls=%async_computation.1 | async-start | bytes 1572864 | tf_op jit(solution)/shard_map/all_to_all | solution.py:215
  68.1 43.5 %copy-start.65 = (bf16[128,512]{0,1:T(8,128)(2,1)}, bf16[128,512]{0,1:T(8,128)(2,1)S(1)}, u32[]{:S(2)}) copy-start(bf16[128,512]{0,1:T(8,128)(2,1)S(1)} %copy.445) | copy-start | bytes 393220
  82.2 20.8 %all-to-all-start.3 = ((s32[16,1,1]{2,1,0:T(1,128)}), s32[16,1,1]{2,1,0:T(1,128)}, u32[]{:S(2)}, u32[]{:S(2)}) async-start(s32[16,1,1]{2,1,0:T(1,128)} %copy.452), calls=%async_computation.3 | async-start | bytes 16384 | tf_op jit(solution)/shard_map/all_to_all | solution.py:222
  103.0 23.6 %all-to-all-start.2 = ((bf16[16,48,512]{2,1,0:T(8,128)(2,1)}), bf16[16,48,512]{2,1,0:T(8,128)(2,1)}, u32[]{:S(2)}, u32[]{:S(2)}) async-start(bf16[16,48,512]{2,1,0:T(8,128)(2,1)} %broadcast_select_fusion.11), calls=%async_computation.2 | async-start | bytes 1572864 | tf_op jit(solution)/shard_map/all_to_all | solution.py:233
  112.6 28.1 %copy-start.85 = (f32[128,2]{1,0:T(8,128)S(1)}, f32[128,2]{1,0:T(8,128)}, u32[]{:S(2)}) copy-start(f32[128,2]{1,0:T(8,128)} %copy.436) | copy-start | bytes 3076
  113.3 40.9 %copy-start.6 = (f32[128,512]{1,0:T(8,128)}, f32[128,512]{1,0:T(8,128)S(1)}, u32[]{:S(2)}) copy-start(f32[128,512]{1,0:T(8,128)S(1)} %convolution_add_fusion.8) | copy-start | bytes 786436
  114.0 21.4 %copy-start.139 = (s32[16,1]{1,0:T(8,128)}, s32[16,1]{1,0:T(8,128)S(1)}, u32[]{:S(2)}) copy-start(s32[16,1]{1,0:T(8,128)S(1)} %reduce-window.35) | copy-start | bytes 196
  115.7 37.7 %copy-start.175 = (s32[16]{0:T(128)}, s32[16]{0:T(128)S(1)}, u32[]{:S(2)}) copy-start(s32[16]{0:T(128)S(1)} %sub.293) | copy-start | bytes 196
  115.7 26.8 %copy-start.158 = (s32[1024]{0:T(1024)}, s32[1024]{0:T(1024)S(1)}, u32[]{:S(2)}) copy-start(s32[1024]{0:T(1024)S(1)} %pad_clamp_fusion.6) | copy-start | bytes 12292
  126.6 39.5 %all-to-all-start.6 = ((s32[16,1,1]{2,1,0:T(1,128)}), s32[16,1,1]{2,1,0:T(1,128)}, u32[]{:S(2)}, u32[]{:S(2)}) async-start(s32[16,1,1]{2,1,0:T(1,128)} %copy.466), calls=%async_computation.6 | async-start | bytes 16384 | tf_op jit(solution)/shard_map/all_to_all | solution.py:222
  151.4 2.8 collective-permute-start
  166.1 22.4 %all-to-all-start.4 = ((bf16[16,48,512]{2,1,0:T(8,128)(2,1)}), bf16[16,48,512]{2,1,0:T(8,128)(2,1)}, u32[]{:S(2)}, u32[]{:S(2)}) async-start(bf16[16,48,512]{2,1,0:T(8,128)(2,1)} %bitcast.678), calls=%async_computation.4 | async-start | bytes 1572864 | tf_op jit(solution)/shard_map/all_to_all | solution.py:215
  202.1 29.0 %all-to-all-start.5 = ((bf16[16,48,512]{2,1,0:T(8,128)(2,1)}), bf16[16,48,512]{2,1,0:T(8,128)(2,1)}, u32[]{:S(2)}, u32[]{:S(2)}) async-start(bf16[16,48,512]{2,1,0:T(8,128)(2,1)} %broadcast_select_fusion.9), calls=%async_computation.5 | async-start | bytes 1572864 | tf_op jit(solution)/shard_map/all_to_all | solution.py:233
  245.6 4.0 collective-permute-start.1
  260.6 22.5 %all-to-all-start.7 = ((bf16[16,48,512]{2,1,0:T(8,128)(2,1)}), bf16[16,48,512]{2,1,0:T(8,128)(2,1)}, u32[]{:S(2)}, u32[]{:S(2)}) async-start(bf16[16,48,512]{2,1,0:T(8,128)(2,1)} %bitcast.679), calls=%async_computation.7 | async-start | bytes 1572864 | tf_op jit(solution)/shard_map/all_to_all | solution.py:215
  296.6 28.3 %all-to-all-start.8 = ((bf16[16,48,512]{2,1,0:T(8,128)(2,1)}), bf16[16,48,512]{2,1,0:T(8,128)(2,1)}, u32[]{:S(2)}, u32[]{:S(2)}) async-start(bf16[16,48,512]{2,1,0:T(8,128)(2,1)} %broadcast_select_fusion.7), calls=%async_computation.8 | async-start | bytes 1572864 | tf_op jit(solution)/shard_map/all_to_all | solution.py:233
  347.5 27.8 %copy-start.146 = (pred[256]{0:T(512)(128)(4,1)S(1)}, pred[256]{0:T(512)(128)(4,1)}, u32[]{:S(2)}) copy-start(pred[256]{0:T(512)(128)(4,1)} %iota_compare_fusion.22) | copy-start | bytes 772
  386.1 21.6 %all-to-all-start.10 = ((bf16[16,48,512]{2,1,0:T(8,128)(2,1)}), bf16[16,48,512]{2,1,0:T(8,128)(2,1)}, u32[]{:S(2)}, u32[]{:S(2)}) async-start(bf16[16,48,512]{2,1,0:T(8,128)(2,1)} %broadcast_select_fusion.6), calls=%async_computation.10 | async-start | bytes 1572864 | tf_op jit(solution)/shard_map/all_to_all | solution.py:375
  423.2 14.2 %collective-permute-start.2 = (bf16[128,1024]{1,0:T(8,128)(2,1)S(1)}, bf16[128,1024]{1,0:T(8,128)(2,1)}, u32[]{:S(2)}, u32[]{:S(2)}) collective-permute-start(bf16[128,1024]{1,0:T(8,128)(2,1)S(1)} %copy.482), channel_id=1, source_target_pairs={{16,0},{17,1},{18,2},{19,3},{20,4},{21,5},{22,6},{23,7},{24,8},{25... | collective-permute-start | bytes 786440 | tf_op jit(solution)/shard_map/ppermute | solution.py:15
  455.9 22.6 %all-to-all-start.11 = ((bf16[16,48,512]{2,1,0:T(8,128)(2,1)}), bf16[16,48,512]{2,1,0:T(8,128)(2,1)}, u32[]{:S(2)}, u32[]{:S(2)}) async-start(bf16[16,48,512]{2,1,0:T(8,128)(2,1)} %bitcast.680), calls=%async_computation.11 | async-start | bytes 1572864 | tf_op jit(solution)/shard_map/all_to_all | solution.py:356
  492.7 17.9 %all-to-all-start.12 = ((bf16[16,48,512]{2,1,0:T(8,128)(2,1)}), bf16[16,48,512]{2,1,0:T(8,128)(2,1)}, u32[]{:S(2)}, u32[]{:S(2)}) async-start(bf16[16,48,512]{2,1,0:T(8,128)(2,1)} %broadcast_select_fusion.8), calls=%async_computation.12 | async-start | bytes 1572864 | tf_op jit(solution)/shard_map/all_to_all | solution.py:375
  527.1 11.5 %collective-permute-start.3 = (bf16[128,1024]{1,0:T(8,128)(2,1)}, bf16[128,1024]{1,0:T(8,128)(2,1)S(1)}, u32[]{:S(2)}, u32[]{:S(2)}) collective-permute-start(bf16[128,1024]{1,0:T(8,128)(2,1)} %copy.494), channel_id=1, source_target_pairs={{16,0},{17,1},{18,2},{19,3},{20,4},{21,5},{22,6},{23,7},{24,8},{25... | collective-permute-start | bytes 786440 | tf_op jit(solution)/shard_map/ppermute | solution.py:15
  555.6 19.3 %all-to-all-start.13 = ((bf16[16,48,512]{2,1,0:T(8,128)(2,1)}), bf16[16,48,512]{2,1,0:T(8,128)(2,1)}, u32[]{:S(2)}, u32[]{:S(2)}) async-start(bf16[16,48,512]{2,1,0:T(8,128)(2,1)} %bitcast.681), calls=%async_computation.13 | async-start | bytes 1572864 | tf_op jit(solution)/shard_map/all_to_all | solution.py:356
  589.1 21.8 %all-to-all-start.14 = ((bf16[16,48,512]{2,1,0:T(8,128)(2,1)}), bf16[16,48,512]{2,1,0:T(8,128)(2,1)}, u32[]{:S(2)}, u32[]{:S(2)}) async-start(bf16[16,48,512]{2,1,0:T(8,128)(2,1)} %broadcast_select_fusion.10), calls=%async_computation.14 | async-start | bytes 1572864 | tf_op jit(solution)/shard_map/all_to_all | solution.py:375
  593.7 276.1 %all-reduce.4.cloned.1.call-start = ((), (), s32[]{:S(2)}) async-start(), calls=%async_computation.15 | async-start | bytes 12582912 | tf_op jit(solution)/shard_map/psum | solution.py:561
  658.4 81.1 %copy-start.203 = (f32[128]{0:T(128)S(1)}, f32[128]{0:T(128)}, u32[]{:S(2)}) copy-start(f32[128]{0:T(128)} %copy-done.202) | copy-start | bytes 1540
  740.7 129.1 %copy-start.91 = (f32[1,2,128,512]{3,2,1,0:T(8,128)}, f32[1,2,128,512]{3,2,1,0:T(8,128)S(1)}, u32[]{:S(2)}) copy-start(f32[1,2,128,512]{3,2,1,0:T(8,128)S(1)} %fusion.235) | copy-start | bytes 1572868
  (194 other events, 1096.3 us)
Sparse Core Ops, SparseCore 0:
  640.7 229.1 all-reduce.3
where the time goes:
time: 898 us; the launch traced here: 884 us
  waiting for transfers between devices  219 us (24%)
  local copies, waits for them, and re-layouts  205 us (23%)
  other arithmetic  117 us (13%)
  matrix products  114 us (13%)
  starting transfers between devices  106 us (12%)
  blocking collectives  103 us (11%)
  between operations  19.7 us (2%)
    psum x1, waiting for transfers between devices, shards(): lax.psum((dense_total[0], dense_total[1], dense_total[2], dense_total[3],...  129 us
    psum x1, blocking collectives, shards(): lax.psum((dense_total[0], dense_total[1], dense_total[2], dense_total[3],...  78.7 us
    dot_general x15, matrix products, contract_rows(): lax.dot_general(left, right, (((0,), (0,)), ((), ())), preferred_element_...  37.2 us
    all_to_all x3, waiting for transfers between devices, layer_forward(): lax.all_to_all(reply_rows.reshape(expert_count, send_rows, model_width),...  32 us
    unnamed x406, local copies, waits for them, and re-layouts  31.8 us
    dot_general x15, matrix products, contract_cols(): lax.dot_general(left, right, (((1,), (1,)), ((), ())), preferred_element_...  27 us
    all_to_all x3, starting transfers between devices, layer_forward(): lax.all_to_all(reply_rows.reshape(expert_count, send_rows, model_width),...  25.4 us
    all_to_all x1, blocking collectives, layer_backward(): lax.all_to_all(outgoing.reshape(expert_count, send_rows, model_width), 'e...  24.5 us
  transfers between devices with their start and end apart: 19, of which 14 were waited for; matrix products, arithmetic and copies ran while one was open for 22% of the time, Pallas kernels for 0%

commit v1 on v0

v1 whole, which is shorter than its diff:
```python
import math
from types import SimpleNamespace

import jax
import jax.numpy as jnp
from jax import lax
from jax.experimental import pallas as pl
from jax.experimental.pallas import tpu as pltpu
from jax.sharding import PartitionSpec as P

HEADS = 8
EPSILON = 1e-06
LANES = 128
MESH = pl.DeviceIdType.MESH
F32 = jnp.float32
BF16 = jnp.bfloat16

SEG, TASK, TABLE, CAPACITY = (0, 2, 4, 5)
INFO_TASK, INFO_RANK, INFO_COUNT = (0, 2, 4)


def round_up(value, unit):
    return -(-value // unit) * unit


def dot(left, right):
    return jnp.dot(left, right, preferred_element_type=F32)


def dot_rows(left, right):
    return lax.dot_general(left, right, (((0,), (0,)), ((), ())), preferred_element_type=F32)


def dot_cols(left, right):
    return lax.dot_general(left, right, (((1,), (1,)), ((), ())), preferred_element_type=F32)


def lane_sum(value):
    return jnp.sum(value, axis=-1, keepdims=True)


def row_sum(value):
    return jnp.sum(value, axis=0, keepdims=True)


def when_equal(left, right, value=1.0):
    return jnp.where(left == right, value, 0.0)


def iota(shape, axis):
    return lax.broadcasted_iota(jnp.int32, shape, axis).astype(F32)


def whole_part(value, unit):
    return jnp.floor((value + 0.5) * (1.0 / unit))


def inverse_rms(value):
    return lax.rsqrt(jnp.mean(value * value, axis=-1, keepdims=True) + EPSILON)


def norm(value, gain):
    return value * inverse_rms(value) * gain


def norm_back(value, gain, grad):
    scale = inverse_rms(value)
    unit = value * scale
    scaled = grad * gain
    grad_value = scale * (scaled - unit * jnp.mean(scaled * unit, axis=-1, keepdims=True))
    return grad_value, row_sum(grad * unit)


def gelu_and_slope(hidden):
    rate = math.sqrt(2.0 / math.pi)
    square = hidden * hidden
    bend = jnp.tanh(hidden * (rate + rate * 0.044715 * square))
    share = 0.5 + 0.5 * bend
    act = hidden * share
    slope = share + act * (1.0 - bend) * (rate + 3.0 * rate * 0.044715 * square)
    return act, slope


class Sizes:
    def __init__(self, inputs, w_qkv, w_cross, w_router, w_up, table, experts):
        _, self.micro, self.tok, self.model = inputs.shape
        self.hidden = w_up.shape[-1]
        self.experts = experts
        self.tasks = table.shape[1]
        self.slots = 2 * self.tok
        self.halves = 2
        self.group = experts // self.halves
        self.bound = max(2, 6 * self.tok // experts)
        self.send = round_up(self.bound, 16)
        self.merged = self.halves * self.bound <= self.send
        self.flights = 1 if self.merged else self.halves
        self.half_rows = self.group * self.send
        self.all_rows = self.flights * self.half_rows
        self.misc = round_up(w_router.shape[-1] + 3, LANES)
        self.qkv_blocks = w_qkv.shape[-1] // LANES
        self.out_blocks = self.model // LANES
        self.cross_blocks = w_cross.shape[-1] // LANES
        self.misc_blocks = self.misc // LANES
        self.blocks = self.qkv_blocks + self.out_blocks + self.cross_blocks + self.misc_blocks
        self.bits = experts.bit_length() - 1
        unit = 16 * experts
        units = -(-self.blocks * self.model // unit)
        share = -(-units // 3)
        self.parts = []
        start = 0
        for part in range(3):
            size = min(share, units - start // unit) * unit
            self.parts.append((start, size))
            start += size
        self.dense_rows = start


def kernel_body(z, names, *refs):
    r = SimpleNamespace(**dict(zip(names, refs)))
    me = lax.axis_index("expert")
    section = lax.axis_index("section")
    is_dec = section == 1
    tok, model, micro, group, send, slots = (z.tok, z.model, z.micro, z.group, z.send, z.slots)
    here = lax.rem(me, group)
    base = me - here
    mirror = lax.rem(me + group, z.experts)
    me_f = me.astype(F32)
    here_f = here.astype(F32)
    base_f = base.astype(F32)
    enc_f = 1.0 - section.astype(F32)

    def enc(run):
        pl.when(section == 0)(run)

    def dec(run):
        pl.when(section == 1)(run)

    loads = [
        pltpu.make_async_copy(source, target, r.load_sem.at[i])
        for i, (source, target) in enumerate(
            (
                (r.w_qkv, r.wqkv),
                (r.w_out, r.wout),
                (r.w_cross, r.wcross),
                (r.w_up, r.wup),
                (r.w_down, r.wdown),
            )
        )
    ]
    for load in loads:
        load.start()

    barrier = pltpu.get_barrier_semaphore()

    def greet(step, _):
        pl.semaphore_signal(
            barrier,
            inc=1,
            device_id={"expert": lax.rem(me + step, z.experts)},
            device_id_type=MESH,
        )
        return 0

    lax.fori_loop(1, z.experts, greet, 0)
    pl.semaphore_signal(
        barrier, inc=1, device_id={"section": 1 - section}, device_id_type=MESH
    )

    meta = r.meta[...].astype(F32)
    meta_cols = jnp.transpose(
        jnp.concatenate([meta, jnp.zeros((LANES - 8, LANES), F32)], axis=0)
    )
    lane = iota((1, LANES), 1)
    earlier = jnp.where(iota((tok, tok), 0) < iota((tok, tok), 1), 1.0, 0.0)
    task_rows, rank_rows, count_rows = ([], [], [])
    for m in range(micro):
        task_col = meta_cols[:, TASK + m : TASK + m + 1]
        task_row = meta[TASK + m : TASK + m + 1, :]
        task_rows.append(task_row)
        rank_rows.append(row_sum(when_equal(task_col, task_row) * earlier))
        count_rows.append(row_sum(when_equal(task_col, lane)))
    r.infos[0] = jnp.concatenate(
        task_rows + rank_rows + count_rows + [jnp.zeros((8 - 3 * micro, LANES), F32)], axis=0
    )

    pl.semaphore_wait(barrier, z.experts)

    def tell(step, _):
        pltpu.make_async_remote_copy(
            src_ref=r.infos.at[0],
            dst_ref=r.infos.at[step],
            send_sem=r.info_send,
            recv_sem=r.info_recv,
            device_id={"expert": lax.rem(me + step, z.experts)},
            device_id_type=MESH,
        ).start()
        return 0

    lax.fori_loop(1, z.experts, tell, 0)

    def settle(ref, sem):
        pltpu.make_async_copy(ref, ref, sem).wait()

    low_lane = jnp.where(iota((1, LANES), 1) < LANES // 2, 1.0, 0.0)
    high_lane = 1.0 - low_lane
    low_bf, high_bf = (low_lane.astype(BF16), high_lane.astype(BF16))
    pairs = model // LANES
    score_scale = (model // HEADS) ** (-0.5)

    def stacked(block):
        return jnp.concatenate([block * low_bf, block * high_bf], axis=0)

    def merged(block):
        return block[:tok] * low_lane + block[tok:] * high_lane

    def attend(queries, keys, values, allowed):
        scores = dot_cols(stacked(queries), keys) * score_scale
        if allowed is not None:
            scores = jnp.where(allowed > 0.5, scores, -1000000000.0)
        top = jnp.max(scores, axis=-1, keepdims=True)
        grown = jnp.exp(scores - top)
        probs = grown / lane_sum(grown)
        return probs, merged(dot(probs.astype(BF16), values))

    def attend_back(queries, keys, values, probs, grad_mixed):
        grad_stack = stacked(grad_mixed)
        grad_probs = dot_cols(grad_stack, values)
        inner = lane_sum(probs * grad_probs)
        grad_scores = (probs * (grad_probs - inner)).astype(BF16)
        grad_queries = merged(dot(grad_scores, keys)) * score_scale
        grad_keys = dot_rows(grad_scores, stacked(queries)) * score_scale
        grad_values = dot_rows(probs.astype(BF16), grad_stack)
        return grad_queries, grad_keys, grad_values

    def cols(index, start=0):
        return pl.ds(start + index * LANES, LANES)

    gains = r.gains[...]
    gain_a, gain_c, gain_m = (gains[0:1], gains[1:2], gains[2:3])

    loads[0].wait()
    loads[1].wait()
    for m in range(micro):
        x_in = r.inputs[m].astype(F32)
        normed_a = norm(x_in, gain_a).astype(BF16)
        r.normed_a[m] = normed_a
        r.qkv[m] = dot(normed_a, r.wqkv[...]).astype(BF16)
        seg_col = meta_cols[:, SEG + m : SEG + m + 1]
        seg_row = meta[SEG + m : SEG + m + 1, :]
        causal = jnp.where(iota((tok, tok), 1) <= iota((tok, tok), 0), 1.0, enc_f)
        allowed = when_equal(seg_col, seg_row) * causal
        allowed = jnp.concatenate([allowed, allowed], axis=0)
        for pair in range(pairs):
            probs, mixed = attend(
                r.qkv[m, :, cols(pair)],
                r.qkv[m, :, cols(pair, model)],
                r.qkv[m, :, cols(pair, 2 * model)],
                allowed,
            )
            r.probs_self[m, pair] = probs
            r.attn_rows[m, :, cols(pair)] = mixed.astype(BF16)
        r.after_self[m] = x_in + dot(r.attn_rows[m], r.wout[...])

    settle(r.infos.at[pl.ds(1, z.experts - 1)], r.info_recv)
    table_row = meta[TABLE : TABLE + 1, :]
    table_task = whole_part(lane, 2)
    own_task = lane_sum(when_equal(table_row, me_f, table_task))
    partner = lane_sum(jnp.where((table_task == own_task) & (table_row >= 0.0), table_row, 0.0)) - me_f
    capacity = meta[CAPACITY : CAPACITY + 1, 0:1]

    line = iota((z.half_rows, 1), 0)
    line_block = whole_part(line, send)
    line_rank = line - line_block * send
    line_place = here_f + line_block
    line_place = jnp.where(line_place >= group, line_place - group, line_place)
    line_task = lane_sum(when_equal(table_row, base_f + line_place, table_task))

    place = iota((1, z.all_rows), 1)
    block = whole_part(place, send)
    place_rank = place - block * send
    place_half = whole_part(block, group)
    sender = here_f - (block - place_half * group)
    if z.merged:
        place_half = jnp.minimum(whole_part(place_rank, z.bound), 1.0)
        place_rank = place_rank - place_half * z.bound
    sender = base_f + jnp.where(sender < 0.0, sender + group, sender) + place_half * group
    sender = jnp.where(sender >= z.experts, sender - z.experts, sender)
    teller = me_f - iota((z.experts, 1), 0)
    teller = jnp.where(teller < 0.0, teller + z.experts, teller)
    own_slot = iota((slots, 1), 0)
    for m in range(micro):
        for half in range(z.halves):
            info = r.infos[half * group]
            hit = (info[INFO_TASK + m : INFO_TASK + m + 1] == line_task) & (
                info[INFO_RANK + m : INFO_RANK + m + 1] == line_rank - (half * z.bound if z.merged else 0)
            )
            r.pick[half, m] = jnp.where(hit, 1.0, 0.0).astype(BF16)
        counts = lane_sum(
            jnp.where(lane == own_task, r.infos[:, INFO_COUNT + m, :], 0.0)
        )
        count = row_sum(when_equal(teller, sender, counts))
        slot = row_sum(jnp.where(teller < sender, counts, 0.0)) + place_rank
        slot = jnp.where((place_rank < count) & (slot < capacity), slot, -1.0)
        r.compact[m] = when_equal(own_slot, slot).astype(BF16)

    def spread(way, m, half, rows, back):
        packed, landed = (
            (r.reply_out, r.reply_in) if back else (r.rows_out, r.rows_in)
        )
        send_sem, recv_sem = (
            (r.reply_send, r.reply_recv) if back else (r.rows_send, r.rows_recv)
        )
        packed[way, m, half] = rows.reshape(group, send, model)
        landed[way, m, half, 0] = rows[:send]

        def push(step, _):
            if back:
                other = lax.rem(here + group - step, group)
            else:
                other = lax.rem(here + step, group)
            pltpu.make_async_remote_copy(
                src_ref=packed.at[way, m, half, step],
                dst_ref=landed.at[way, m, half, step],
                send_sem=send_sem.at[way, m, half],
                recv_sem=recv_sem.at[way, m, half],
                device_id={"expert": base + other},
                device_id_type=MESH,
            ).start()
            return 0

        lax.fori_loop(1, group, push, 0)

    def swap(source, target, send_sem, recv_sem):
        return pltpu.make_async_remote_copy(
            src_ref=source,
            dst_ref=target,
            send_sem=send_sem,
            recv_sem=recv_sem,
            device_id={"expert": mirror},
            device_id_type=MESH,
        )

    def swap_rows(way, m, source):
        return swap(
            source.at[m], r.mirror_rows.at[way, m], r.mirror_send.at[way, m], r.mirror_recv.at[way, m]
        )

    def swap_sums(way, m):
        return swap(
            r.sums_out.at[way, m], r.sums_in.at[way, m], r.sums_send.at[way, m], r.sums_recv.at[way, m]
        )

    def dispatch(way, m, source):
        swap_rows(way, m, source).start()
        if not z.merged:
            spread(way, m, 0, dot(r.pick[0, m], source[m]).astype(BF16), False)

    def dispatch_mirror(way, m, source):
        swap_rows(way, m, source).wait_recv()
        rows = dot(r.pick[1, m], r.mirror_rows[way, m])
        if z.merged:
            rows += dot(r.pick[0, m], source[m])
        spread(way, m, z.flights - 1, rows.astype(BF16), False)

    def arrived(way, m):
        for half in range(z.flights):
            settle(r.rows_in.at[way, m, half, pl.ds(1, group - 1)], r.rows_recv.at[way, m, half])
        return dot(r.compact[m], r.rows_in[way, m].reshape(z.all_rows, model))

    def combine(way, m, rows):
        reply = dot_rows(r.compact[m], rows).astype(BF16)
        for half in reversed(range(z.flights)):
            spread(way, m, half, reply[half * z.half_rows : (half + 1) * z.half_rows], True)

    def gathered(way, m, half):
        flight = 0 if z.merged else half
        if not z.merged or half == 1:
            settle(r.reply_in.at[way, m, flight, pl.ds(1, group - 1)], r.reply_recv.at[way, m, flight])
        return dot_rows(r.pick[half, m], r.reply_in[way, m, flight].reshape(z.half_rows, model))

    def combine_mirror(way, m):
        r.sums_out[way, m] = gathered(way, m, 1).astype(BF16)
        swap_sums(way, m).start()

    def combine_end(way, m):
        own = gathered(way, m, 0)
        swap_sums(way, m).wait_recv()
        return own + r.sums_in[way, m].astype(F32)

    @dec
    def _():
        for m in range(micro):
            dispatch(1, m, r.cotangent)
        for m in range(micro):
            dispatch_mirror(1, m, r.cotangent)

    loads[2].wait()

    def memory_copy(m):
        return pltpu.make_async_remote_copy(
            src_ref=r.memory_out.at[m],
            dst_ref=r.memory.at[m],
            send_sem=r.memory_send.at[m],
            recv_sem=r.memory_recv.at[m],
            device_id={"section": 1 - section},
            device_id_type=MESH,
        )

    def grad_memory_copy(m):
        return pltpu.make_async_remote_copy(
            src_ref=r.memory_out.at[m],
            dst_ref=r.memory.at[m],
            send_sem=r.memory_send.at[micro + m],
            recv_sem=r.memory_recv.at[micro + m],
            device_id={"section": 1 - section},
            device_id_type=MESH,
        )

    for m in range(micro):

        @enc
        def _():
            r.after_cross[m] = r.after_self[m]

        @dec
        def _():
            after_self = r.after_self[m]
            normed_c = norm(after_self, gain_c).astype(BF16)
            r.normed_c[m] = normed_c
            r.cross_q[m] = dot(normed_c, r.wcross[:, :model]).astype(BF16)
            memory_copy(m).wait_recv()
            for pair in range(pairs):
                probs, mixed = attend(
                    r.cross_q[m, :, cols(pair)],
                    r.memory[m, :, cols(pair)],
                    r.memory[m, :, cols(pair, model)],
                    None,
                )
                r.probs_cross[m, pair] = probs
                r.cross_rows[m, :, cols(pair)] = mixed.astype(BF16)
            r.after_cross[m] = after_self + dot_cols(r.cross_rows[m], r.wcross[:, model:])

        r.normed_m[m] = norm(r.after_cross[m], gain_m).astype(BF16)
        dispatch(0, m, r.normed_m)
    for m in range(micro):
        dispatch_mirror(0, m, r.normed_m)

    router = r.w_router[...]
    expert_lane = iota((8, router.shape[-1]), 1)
    sign = when_equal(expert_lane, me_f) - when_equal(expert_lane, partner)
    router_step = dot_cols(sign.astype(BF16), router)[0:1]
    tile = 256
    loads[3].wait()
    loads[4].wait()
    for m in range(micro):
        taken = arrived(0, m).astype(BF16)
        r.taken[m] = taken

        def up_tile(index, _):
            at = pl.ds(pl.multiple_of(index * tile, tile), tile)
            hidden = dot(r.taken[m], r.wup[:, at])
            act, slope = gelu_and_slope(hidden)
            r.act[m, :, at] = act.astype(BF16)
            r.slope[m, :, at] = slope.astype(BF16)
            return 0

        lax.fori_loop(0, z.hidden // tile, up_tile, 0)
        gap = lane_sum(taken.astype(F32) * router_step)
        small = jnp.exp(-jnp.abs(gap))
        large = 1.0 / (1.0 + small)
        gate = jnp.where(gap >= 0.0, large, small * large)
        r.gate[m] = gate
        r.gate_slope[m] = small * large * large

        def down_tile(index, _):
            at = pl.ds(pl.multiple_of(index * tile, tile), tile)
            r.expert_out[m, :, at] = dot(r.act[m], r.wdown[:, at]).astype(BF16)
            return 0

        lax.fori_loop(0, model // tile, down_tile, 0)
        r.gated[m] = (gate * r.expert_out[m].astype(F32)).astype(BF16)

        @enc
        def _():
            combine(0, m, r.gated[m])

    @enc
    def _():
        for m in range(micro):
            combine_mirror(0, m)
        for m in range(micro):
            layer_final = r.after_cross[m] + combine_end(0, m)
            r.layer_final[m] = layer_final
            r.layer_out[m] = layer_final.astype(BF16)
            normed_k = norm(layer_final, gain_c).astype(BF16)
            r.normed_c[m] = normed_k
            r.memory_out[m] = dot(normed_k, r.wcross[...]).astype(BF16)
            memory_copy(m).start()
        gain_grad = jnp.zeros((1, model), F32)
        for m in range(micro):
            grad_memory_copy(m).wait_recv()
            grad_normed = dot_cols(r.memory[m], r.wcross[...])
            grad_state, grad_gain = norm_back(r.layer_final[m], gain_c, grad_normed)
            gain_grad += grad_gain
            grad_final = r.cotangent[m].astype(F32) + grad_state
            r.grad_state[m] = grad_final
            r.grad_rows[m] = grad_final.astype(BF16)
            dispatch(1, m, r.grad_rows)
        for m in range(micro):
            dispatch_mirror(1, m, r.grad_rows)
        r.gain_grads[1:2] = gain_grad

    @dec
    def _():
        for m in range(micro):
            r.grad_state[m] = r.cotangent[m].astype(F32)

    for m in range(micro):
        grad_final = arrived(1, m)
        grad_gate = lane_sum(r.expert_out[m].astype(F32) * grad_final)
        grad_gap = r.gate_slope[m] * grad_gate
        r.grad_gap[m] = grad_gap
        r.grad_out[m] = (r.gate[m] * grad_final).astype(BF16)

        def act_tile(index, _):
            at = pl.ds(pl.multiple_of(index * tile, tile), tile)
            grad_act = dot_cols(r.grad_out[m], r.wdown[at, :])
            r.grad_hidden[m, :, at] = (grad_act * r.slope[m, :, at].astype(F32)).astype(BF16)
            return 0

        lax.fori_loop(0, z.hidden // tile, act_tile, 0)

        def taken_tile(index, _):
            at = pl.ds(pl.multiple_of(index * tile, tile), tile)
            r.grad_taken[:, at] = dot_cols(r.grad_hidden[m], r.wup[at, :])
            return 0

        lax.fori_loop(0, model // tile, taken_tile, 0)
        rounded = r.grad_taken[...].astype(BF16).astype(F32)
        combine(1, m, (rounded + grad_gap * router_step).astype(BF16))
    for m in range(micro):
        combine_mirror(1, m)

    @dec
    def _():
        for m in range(micro):
            combine(0, m, r.gated[m])

    gain_grad = jnp.zeros((1, model), F32)
    for m in range(micro):
        grad_state, grad_gain = norm_back(r.after_cross[m], gain_m, combine_end(1, m))
        gain_grad += grad_gain
        r.grad_state[m] += grad_state

        @dec
        def _():
            grad_y = r.grad_state[m].astype(BF16)
            r.grad_cross[m] = grad_y
            grad_mix = dot(grad_y, r.wcross[:, model:]).astype(BF16)
            for pair in range(pairs):
                at = cols(pair)
                grad_q, grad_k, grad_v = attend_back(
                    r.cross_q[m, :, at],
                    r.memory[m, :, at],
                    r.memory[m, :, cols(pair, model)],
                    r.probs_cross[m, pair],
                    grad_mix[:, pair * LANES : (pair + 1) * LANES],
                )
                r.grad_cross_q[m, :, at] = grad_q.astype(BF16)
                r.memory_out[m, :, at] = grad_k.astype(BF16)
                r.memory_out[m, :, cols(pair, model)] = grad_v.astype(BF16)
            grad_memory_copy(m).start()

    r.gain_grads[2:3] = gain_grad

    @dec
    def _():
        gain_grad = jnp.zeros((1, model), F32)
        for m in range(micro):
            grad_normed = dot_cols(r.grad_cross_q[m], r.wcross[:, :model])
            grad_state, grad_gain = norm_back(r.after_self[m], gain_c, grad_normed)
            gain_grad += grad_gain
            r.grad_state[m] += grad_state
        r.gain_grads[1:2] = gain_grad
        for m in range(micro):
            combine_mirror(0, m)
        for m in range(micro):
            r.layer_out[m] = (r.after_cross[m] + combine_end(0, m)).astype(BF16)

    gain_grad = jnp.zeros((1, model), F32)
    for m in range(micro):
        grad_top = r.grad_state[m]
        grad_y = grad_top.astype(BF16)
        r.grad_self[m] = grad_y
        grad_mix = dot_cols(grad_y, r.wout[...]).astype(BF16)
        for pair in range(pairs):
            grads = attend_back(
                r.qkv[m, :, cols(pair)],
                r.qkv[m, :, cols(pair, model)],
                r.qkv[m, :, cols(pair, 2 * model)],
                r.probs_self[m, pair],
                grad_mix[:, pair * LANES : (pair + 1) * LANES],
            )
            for third, grad in enumerate(grads):
                r.grad_qkv[m, :, cols(pair, third * model)] = grad.astype(BF16)
        grad_normed = dot_cols(r.grad_qkv[m], r.wqkv[...])
        grad_state, grad_gain = norm_back(r.inputs[m].astype(F32), gain_a, grad_normed)
        gain_grad += grad_gain
        r.inputs_grad[m] = grad_top + grad_state
    r.gain_grads[0:1] = gain_grad
    r.gain_grads[3:8] = jnp.zeros((5, model), F32)

    def flat(ref):
        return ref[...].reshape(micro * tok, ref.shape[-1])

    def store_blocks(first, left, right):
        width = 2 * LANES
        left = flat(left)
        for start in range(0, right.shape[-1], width):
            part = dot_rows(left, right[:, :, start : start + width].reshape(micro * tok, width))
            at = (first + start // LANES) * model
            r.dense[at : at + model] = part[:, :LANES].astype(BF16)
            r.dense[at + model : at + 2 * model] = part[:, LANES:].astype(BF16)

    first_out = z.qkv_blocks
    first_cross = first_out + z.out_blocks
    first_misc = first_cross + z.cross_blocks
    store_blocks(0, r.normed_a, r.grad_qkv)
    store_blocks(first_out, r.attn_rows, r.grad_self)

    @enc
    def _():
        store_blocks(first_cross, r.normed_c, r.memory)

    @dec
    def _():
        store_blocks(first_cross, r.normed_c, r.grad_cross_q)
        store_blocks(first_cross + z.out_blocks, r.grad_cross, r.cross_rows)

    misc_lane = iota((1, z.misc), 1)
    misc_sign = when_equal(misc_lane, me_f) - when_equal(misc_lane, partner)
    misc = jnp.zeros((model, z.misc), F32)
    for m in range(micro):
        steps = r.grad_gap[m] * misc_sign
        top = steps.astype(BF16)
        rest = (steps - top.astype(F32)).astype(BF16)
        misc += dot_rows(r.taken[m], top) + dot_rows(r.taken[m], rest)
    place_gain = when_equal(iota((8, z.misc), 1), iota((8, z.misc), 0) + router.shape[-1])
    misc += dot_rows(r.gain_grads[...].astype(BF16), place_gain.astype(BF16))
    for index in range(z.misc_blocks):
        at = (first_misc + index) * model
        r.dense[at : at + model] = misc[:, index * LANES : (index + 1) * LANES].astype(BF16)
    used = z.blocks * model
    if used < z.dense_rows:
        r.dense[used:] = jnp.zeros((z.dense_rows - used, LANES), BF16)

    saves = [
        pltpu.make_async_copy(source, target, r.load_sem.at[i])
        for i, (source, target) in enumerate(
            (
                (r.taken, r.taken_out),
                (r.grad_hidden, r.grad_hidden_out),
                (r.act, r.act_out),
                (r.grad_out, r.grad_out_out),
            )
        )
    ]
    for save in saves:
        save.start()

    bits = list(range(z.bits))
    lead = min(3, z.bits)
    orders = [bits[:lead][p % lead :] + bits[:lead][: p % lead] + bits[lead:] for p in range(3)]
    offs = [jnp.int32(start) for start, _ in z.parts]
    sizes = [size for _, size in z.parts]
    lands = [start for start, _ in z.parts]

    def aligned(start, size):
        return pl.ds(pl.multiple_of(start, 16), size)

    def other_of(part, step):
        stride = 1 << orders[part][step]
        bit = lax.rem(lax.div(me, stride), 2)
        return bit, me + (1 - 2 * bit) * stride

    def exchange(part, step, source_ref, source, target, target_ref, stage):
        _, other = other_of(part, step)
        return pltpu.make_async_remote_copy(
            src_ref=source_ref.at[source],
            dst_ref=target_ref.at[target],
            send_sem=r.sum_send.at[part, stage],
            recv_sem=r.sum_recv.at[part, stage],
            device_id={"expert": other},
            device_id_type=MESH,
        )

    flights = [None] * 3

    def start_halving(part, step):
        bit, _ = other_of(part, step)
        half = sizes[part] // 2
        give = offs[part] + (1 - bit) * half
        keep = offs[part] + bit * half
        landing = pl.ds(lands[part], half)
        copy = exchange(part, step, r.dense, aligned(give, half), landing, r.partial, step)
        copy.start()
        offs[part] = keep
        sizes[part] = half
        lands[part] += half
        flights[part] = (copy, landing)

    def end_halving(part):
        copy, landing = flights[part]
        copy.wait()
        at = aligned(offs[part], sizes[part])
        target = r.dense if sizes[part] > z.parts[part][1] >> z.bits else r.total
        target[at] = (r.dense[at].astype(F32) + r.partial[landing].astype(F32)).astype(BF16)

    def start_doubling(part, step):
        at = aligned(offs[part], sizes[part])
        copy = exchange(part, step, r.total, at, at, r.total, z.bits + step)
        copy.start()
        flights[part] = copy

    def end_doubling(part, step):
        flights[part].wait()
        bit, _ = other_of(part, step)
        offs[part] = offs[part] - bit * sizes[part]
        sizes[part] *= 2

    live = [part for part in range(3) if sizes[part] > 0]
    for step in range(z.bits):
        for part in live:
            if step > 0:
                end_halving(part)
            start_halving(part, step)
    for step in reversed(range(z.bits)):
        for part in live:
            if step == z.bits - 1:
                end_halving(part)
            else:
                end_doubling(part, step + 1)
            start_doubling(part, step)
    for part in live:
        end_doubling(part, 0)

    dense_save = pltpu.make_async_copy(r.total, r.dense_out, r.load_sem.at[4])
    dense_save.start()
    for save in saves:
        save.wait()
    dense_save.wait()

    settle(r.infos.at[pl.ds(1, z.experts - 1)], r.info_send)
    for way in range(2):
        for m in range(micro):
            for half in range(z.flights):
                others = pl.ds(1, group - 1)
                settle(r.rows_out.at[way, m, half, others], r.rows_send.at[way, m, half])
                settle(r.reply_out.at[way, m, half, others], r.reply_send.at[way, m, half])
            settle(r.mirror_rows.at[way, m], r.mirror_send.at[way, m])
            settle(r.sums_out.at[way, m], r.sums_send.at[way, m])

    @enc
    def _():
        for m in range(micro):
            memory_copy(m).wait_send()

    @dec
    def _():
        for m in range(micro):
            grad_memory_copy(m).wait_send()


def run_kernel(z, meta, arrays):
    micro, tok, model, hidden = (z.micro, z.tok, z.model, z.hidden)
    vmem = pl.BlockSpec(memory_space=pltpu.VMEM)
    hbm = pl.BlockSpec(memory_space=pl.ANY)
    inputs = dict(
        meta=(meta, vmem),
        inputs=(arrays.inputs, vmem),
        cotangent=(arrays.cotangent, vmem),
        gains=(arrays.gains, vmem),
        w_router=(arrays.w_router, vmem),
        w_qkv=(arrays.w_qkv, hbm),
        w_out=(arrays.w_out, hbm),
        w_cross=(arrays.w_cross, hbm),
        w_up=(arrays.w_up, hbm),
        w_down=(arrays.w_down, hbm),
    )
    rows = (micro, tok, model)
    slot_rows = (micro, z.slots, model)
    slot_hidden = (micro, z.slots, hidden)
    outputs = dict(
        layer_out=(rows, BF16, vmem),
        inputs_grad=(rows, F32, vmem),
        dense_out=((z.dense_rows, LANES), BF16, hbm),
        taken_out=(slot_rows, BF16, hbm),
        grad_hidden_out=(slot_hidden, BF16, hbm),
        act_out=(slot_hidden, BF16, hbm),
        grad_out_out=(slot_rows, BF16, hbm),
    )
    blocks = (2, micro, z.flights, z.group, z.send, model)
    pairs = model // LANES
    dma = pltpu.SemaphoreType.DMA
    scratch = dict(
        wqkv=pltpu.VMEM(arrays.w_qkv.shape, BF16),
        wout=pltpu.VMEM(arrays.w_out.shape, BF16),
        wcross=pltpu.VMEM(arrays.w_cross.shape, BF16),
        wup=pltpu.VMEM(arrays.w_up.shape, BF16),
        wdown=pltpu.VMEM(arrays.w_down.shape, BF16),
        infos=pltpu.VMEM((z.experts, 8, LANES), F32),
        normed_a=pltpu.VMEM(rows, BF16),
        qkv=pltpu.VMEM((micro, tok, 3 * model), BF16),
        probs_self=pltpu.VMEM((micro, pairs, 2 * tok, tok), F32),
        attn_rows=pltpu.VMEM(rows, BF16),
        after_self=pltpu.VMEM(rows, F32),
        normed_c=pltpu.VMEM(rows, BF16),
        cross_q=pltpu.VMEM(rows, BF16),
        probs_cross=pltpu.VMEM((micro, pairs, 2 * tok, tok), F32),
        cross_rows=pltpu.VMEM(rows, BF16),
        memory_out=pltpu.VMEM((micro, tok, 2 * model), BF16),
        memory=pltpu.VMEM((micro, tok, 2 * model), BF16),
        after_cross=pltpu.VMEM(rows, F32),
        normed_m=pltpu.VMEM(rows, BF16),
        layer_final=pltpu.VMEM(rows, F32),
        grad_state=pltpu.VMEM(rows, F32),
        grad_rows=pltpu.VMEM(rows, BF16),
        grad_cross=pltpu.VMEM(rows, BF16),
        grad_cross_q=pltpu.VMEM(rows, BF16),
        grad_self=pltpu.VMEM(rows, BF16),
        grad_qkv=pltpu.VMEM((micro, tok, 3 * model), BF16),
        gain_grads=pltpu.VMEM((8, model), F32),
        pick=pltpu.VMEM((z.halves, micro, z.half_rows, tok), BF16),
        compact=pltpu.VMEM((micro, z.slots, z.all_rows), BF16),
        rows_out=pltpu.VMEM(blocks, BF16),
        rows_in=pltpu.VMEM(blocks, BF16),
        reply_out=pltpu.VMEM(blocks, BF16),
        reply_in=pltpu.VMEM(blocks, BF16),
        mirror_rows=pltpu.VMEM((2,) + rows, BF16),
        sums_out=pltpu.VMEM((2,) + rows, BF16),
        sums_in=pltpu.VMEM((2,) + rows, BF16),
        taken=pltpu.VMEM(slot_rows, BF16),
        slope=pltpu.VMEM(slot_hidden, BF16),
        act=pltpu.VMEM(slot_hidden, BF16),
        expert_out=pltpu.VMEM(slot_rows, BF16),
        gated=pltpu.VMEM(slot_rows, BF16),
        gate=pltpu.VMEM((micro, z.slots, 1), F32),
        gate_slope=pltpu.VMEM((micro, z.slots, 1), F32),
        grad_gap=pltpu.VMEM((micro, z.slots, 1), F32),
        grad_out=pltpu.VMEM(slot_rows, BF16),
        grad_hidden=pltpu.VMEM(slot_hidden, BF16),
        grad_taken=pltpu.VMEM((z.slots, model), F32),
        dense=pltpu.VMEM((z.dense_rows, LANES), BF16),
        total=pltpu.VMEM((z.dense_rows, LANES), BF16),
        partial=pltpu.VMEM((z.dense_rows, LANES), BF16),
        load_sem=dma((5,)),
        info_send=dma(()),
        info_recv=dma(()),
        rows_send=dma((2, micro, z.flights)),
        rows_recv=dma((2, micro, z.flights)),
        reply_send=dma((2, micro, z.flights)),
        reply_recv=dma((2, micro, z.flights)),
        mirror_send=dma((2, micro)),
        mirror_recv=dma((2, micro)),
        sums_send=dma((2, micro)),
        sums_recv=dma((2, micro)),
        memory_send=dma((2 * micro,)),
        memory_recv=dma((2 * micro,)),
        sum_send=dma((3, 2 * z.bits)),
        sum_recv=dma((3, 2 * z.bits)),
    )
    names = [*inputs, *outputs, *scratch]

    def body(*refs):
        kernel_body(z, names, *refs)

    return pl.pallas_call(
        body,
        name="layer_step",
        out_shape=[jax.ShapeDtypeStruct(shape, dtype) for shape, dtype, _ in outputs.values()],
        in_specs=[spec for _, spec in inputs.values()],
        out_specs=[spec for _, _, spec in outputs.values()],
        scratch_shapes=list(scratch.values()),
        compiler_params=pltpu.CompilerParams(
            collective_id=0, has_side_effects=True, vmem_limit_bytes=62 * 1024 * 1024
        ),
    )(*[value for value, _ in inputs.values()])


def shards(
    inputs,
    cotangent,
    segments,
    tasks,
    table,
    capacity,
    gains,
    w_qkv,
    w_out,
    w_cross,
    w_router,
    w_up,
    w_down,
):
    experts = lax.axis_size("expert")
    z = Sizes(inputs, w_qkv, w_cross, w_router, w_up, table, experts)
    model = z.model
    table_flat = table.reshape(1, 2 * z.tasks)
    meta = jnp.concatenate(
        [
            segments[0],
            tasks[0, :, :, 0],
            jnp.pad(table_flat, ((0, 0), (0, LANES - 2 * z.tasks)), constant_values=-1),
            jnp.broadcast_to(capacity.reshape(1, 1), (1, LANES)),
            jnp.zeros((2, LANES), jnp.int32),
        ],
        axis=0,
    )
    arrays = SimpleNamespace(
        inputs=inputs[0],
        cotangent=cotangent[0],
        gains=gains[0],
        w_router=w_router[0],
        w_qkv=w_qkv[0],
        w_out=w_out[0],
        w_cross=w_cross[0],
        w_up=w_up[0, 0],
        w_down=w_down[0, 0],
    )
    layer_out, inputs_grad, dense, taken, grad_hidden, act, grad_out = run_kernel(z, meta, arrays)

    def rows_of(value):
        return value.reshape(z.micro * z.slots, value.shape[-1])

    grad_up = dot_rows(rows_of(taken), rows_of(grad_hidden))
    grad_down = dot_rows(rows_of(act), rows_of(grad_out))

    def blocks_of(first, count):
        part = dense[first * model : (first + count) * model].reshape(count, model, LANES)
        return part.transpose(1, 0, 2).reshape(model, count * LANES).astype(F32)

    first_out = z.qkv_blocks
    first_cross = first_out + z.out_blocks
    first_misc = first_cross + z.cross_blocks
    misc = blocks_of(first_misc, z.misc_blocks)
    routers = w_router.shape[-1]
    return (
        layer_out[None],
        inputs_grad[None],
        misc[:, routers : routers + 3].T[None],
        blocks_of(0, z.qkv_blocks)[None],
        blocks_of(first_out, z.out_blocks)[None],
        blocks_of(first_cross, z.cross_blocks)[None],
        misc[:, :routers][None],
        grad_up[None, None],
        grad_down[None, None],
    )


def solution(mesh):
    in_specs = (
        P("section", None, "expert", None),
        P("section", None, "expert", None),
        P("section", None, "expert"),
        P("section", None, "expert", None),
        P("section", None, None),
        P("section"),
        P("section", None, None),
        P("section", None, None),
        P("section", None, None),
        P("section", None, None),
        P("section", None, None),
        P("section", "expert", None, None),
        P("section", "expert", None, None),
    )
    out_specs = (
        P("section", None, "expert", None),
        P("section", None, "expert", None),
        P("section", None, None),
        P("section", None, None),
        P("section", None, None),
        P("section", None, None),
        P("section", None, None),
        P("section", "expert", None, None),
        P("section", "expert", None, None),
    )
    return jax.shard_map(shards, mesh=mesh, in_specs=in_specs, out_specs=out_specs, check_vma=False)
```

time: 898 us -> 234 us (0.26); the launches traced: 884 us -> 233 us
  waiting for transfers between devices: 219 us -> 0 us
  Pallas kernels: 0 us -> 201 us
  local copies, waits for them, and re-layouts: 205 us -> 21.9 us
  other arithmetic: 117 us -> 1.13 us
  starting transfers between devices: 106 us -> 0 us
  matrix products: 114 us -> 8.51 us
  blocking collectives: 103 us -> 0 us
  between operations: 19.7 us -> 1.39 us
    pallas_call x0 -> x1, Pallas kernels: none -> 201 us  [run_kernel(): pl.pallas_call(body, name='layer_step', out_shape=[jax.ShapeDtypeStruct(s...]
    psum x1 -> x0, waiting for transfers between devices: 129 us -> none  [shards(): lax.psum((dense_total[0], dense_total[1], dense_total[2], dense_total[3],...]
    dot_general x71 -> x2, matrix products: 114 us -> 8.51 us  [dot_rows(): lax.dot_general(left, right, (((0,), (0,)), ((), ())), preferred_element_...]
    all_to_all x14 -> x0, starting transfers between devices: 99 us -> none  [the longest x3 25.4 us: layer_forward(): lax.all_to_all(reply_rows.reshape(expert_count, send_rows, model_width),...]
    psum x1 -> x0, blocking collectives: 78.7 us -> none  [shards(): lax.psum((dense_total[0], dense_total[1], dense_total[2], dense_total[3],...]
    all_to_all x14 -> x0, waiting for transfers between devices: 71.4 us -> none  [the longest x3 32 us: layer_forward(): lax.all_to_all(reply_rows.reshape(expert_count, send_rows, model_width),...]
    gather x33 -> x0, local copies, waits for them, and re-layouts: 63.3 us -> none  [the longest x3 10.2 us: layer_forward(): reply_rows = jnp.where(row_live[:, None], result[row_slot], 0)]
    reduce_sum x38 -> x0, other arithmetic: 27 us -> none  [the longest x10 7.92 us: rms_norm(): jnp.mean(value * value, axis=-1, keepdims=True) + EPSILON]
  transfers between devices with their start and end apart: 19 -> 0, of which waited for: 14 -> 0; matrix products, arithmetic and copies ran while one was open for 22% -> 0% of each run, Pallas kernels for 0% -> 0%
where the time goes in v1:
time: 234 us; the launch traced here: 233 us
  Pallas kernels  201 us (86%)
  local copies, waits for them, and re-layouts  21.9 us (9%)
  matrix products  8.51 us (4%)
    pallas_call x1, Pallas kernels, run_kernel(): pl.pallas_call(body, name='layer_step', out_shape=[jax.ShapeDtypeStruct(s...  201 us
    unnamed x16, local copies, waits for them, and re-layouts  8.83 us
    dot_general x2, matrix products, dot_rows(): lax.dot_general(left, right, (((0,), (0,)), ((), ())), preferred_element_...  8.51 us
    convert_element_type x5, local copies, waits for them, and re-layouts, blocks_of(): return part.transpose(1, 0, 2).reshape(model, count * LANES).astype(F32)  6.48 us
    slice x3, local copies, waits for them, and re-layouts, blocks_of(): dense[first * model:(first + count) * model].reshape(count, model, LANES)  5.02 us

profile of v1, /device:TPU:0, one launch (start us, length us, event | category | flops | bytes accessed | tf_op | source)
XLA Modules:
  0.0 233.4 jit_solution(2784081309991373812)
XLA Ops:
  1.3 0.8 copy.31
  2.1 0.1 reshape.77
  2.2 1.3 concatenate.3.refs_0_
  3.5 1.3 copy.45
  4.7 1.5 copy.32
  6.2 200.5 %layer_step.1 = (bf16[2,128,512]{2,1,0:T(8,128)(2,1)}, f32[2,128,512]{2,1,0:T(8,128)}, bf16[12800,128]{1,0:T(8,128)(2,1)}, bf16[2,256,512]{2,1,0:T(8,128)(2,1)},...) custom-call(s32[8,128]{1,0:T(8,128)} %concatenate.3.refs_0_, ...), custom_call_target="tpu_custom_call" | custom-call | tf_op jit(solution)/shard_map/layer_step/pallas_call | solution.py:877
  206.8 0.9 slice_convert_fusion
  207.7 0.7 copy.40
  208.4 0.1 slice_bitcast_fusion.1
  208.6 0.7 copy.38
  209.3 1.1 slice.21
  210.4 0.1 convert_bitcast_fusion.1
  210.4 0.7 copy.34
  211.1 1.4 reshape.79
  212.5 1.3 slice.22
  213.8 2.7 %slice.20 = bf16[6144,128]{1,0:T(8,128)(2,1)} slice(bf16[12800,128]{1,0:T(8,128)(2,1)} %get-tuple-element.18), slice={[0:6144], [0:128]} | slice | bytes 3145728 | tf_op jit(solution)/shard_map/slice | solution.py:939
  216.5 0.1 convert_bitcast_fusion
  216.6 1.2 copy.35
  217.8 1.5 reshape.80
  219.3 1.7 copy.33
  221.0 2.4 %copy.39 = f32[1,512,1536]{2,1,0:T(8,128)} copy(f32[1,512,1536]{1,2,0:T(8,128)S(1)} %bitcast.48) | data formatting | bytes 6291456
  223.4 0.0 copy-start.2
  223.4 0.0 copy-start.3
  223.4 5.2 %convolution_bitcast_fusion.1 = f32[1,1,512,2048]{3,2,1,0:T(8,128)} fusion(bf16[2,256,512]{2,1,0:T(8,128)(2,1)} %get-tuple-element.19, bf16[2,256,2048]{2,1,0:T(8,128)(2,1)} %get-tuple-element.20), kind=kOutput, calls=%fused_computation.1 | convolution fusion | flops 1073741824 | bytes 6815744 | tf_op jit(solution)/shard_map/dot_general | solution.py:31
  228.6 0.0 copy-done.2
  228.6 0.0 copy-done.3
  228.6 0.0 copy-start
  228.6 3.3 %convolution_bitcast_fusion = f32[1,1,2048,512]{3,2,1,0:T(8,128)} fusion(bf16[2,256,2048]{2,1,0:T(8,128)(2,1)S(1)} %copy-done.2, bf16[2,256,512]{2,1,0:T(8,128)(2,1)S(1)} %copy-done.3), kind=kOutput, calls=%fused_computation | convolution fusion | flops 1073741824 | bytes 6815744 | tf_op jit(solution)/shard_map/dot_general | solution.py:31
  231.9 0.0 copy-done.1
  231.9 0.7 copy.49
  232.6 0.0 copy-done
  232.7 0.8 copy.50
  (5 shorter events, 0.0 us)
Async XLA Ops:
  223.4 5.2 %copy-start.2 = (bf16[2,256,2048]{2,1,0:T(8,128)(2,1)S(1)}, bf16[2,256,2048]{2,1,0:T(8,128)(2,1)}, u32[]{:S(2)}) copy-start(bf16[2,256,2048]{2,1,0:T(8,128)(2,1)} %get-tuple-element.21) | copy-start | bytes 6291460
  223.4 5.2 %copy-start.3 = (bf16[2,256,512]{2,1,0:T(8,128)(2,1)S(1)}, bf16[2,256,512]{2,1,0:T(8,128)(2,1)}, u32[]{:S(2)}) copy-start(bf16[2,256,512]{2,1,0:T(8,128)(2,1)} %get-tuple-element.22) | copy-start | bytes 1572868
  228.6 3.3 %copy-start.1 = (bf16[2,128,512]{2,1,0:T(8,128)(2,1)S(1)}, bf16[2,128,512]{2,1,0:T(8,128)(2,1)}, u32[]{:S(2)}) copy-start(bf16[2,128,512]{2,1,0:T(8,128)(2,1)} %get-tuple-element.16) | copy-start | bytes 786436
  228.6 4.0 %copy-start = (f32[2,128,512]{2,1,0:T(8,128)S(1)}, f32[2,128,512]{2,1,0:T(8,128)}, u32[]{:S(2)}) copy-start(f32[2,128,512]{2,1,0:T(8,128)} %get-tuple-element.17) | copy-start | bytes 1572868

commit v2 on v1

v2 whole, which is shorter than its diff:
```python
import math
from types import SimpleNamespace

import jax
import jax.numpy as jnp
from jax import lax
from jax.experimental import pallas as pl
from jax.experimental.pallas import tpu as pltpu
from jax.sharding import PartitionSpec as P

HEADS = 8
EPSILON = 1e-06
LANES = 128
UNROLL = 4
MESH = pl.DeviceIdType.MESH
F32 = jnp.float32
BF16 = jnp.bfloat16

INFO_TASK, INFO_RANK, INFO_COUNT = (0, 2, 4)
ROWS, REPLY, MIRROR, SUMS, MEMORY, SENT = (1000, 2000, 3000, 4000, 5000, 10000)


def round_up(value, unit):
    return -(-value // unit) * unit


def dot(left, right):
    return jnp.dot(left, right, preferred_element_type=F32)


def dot_rows(left, right):
    return lax.dot_general(left, right, (((0,), (0,)), ((), ())), preferred_element_type=F32)


def dot_cols(left, right):
    return lax.dot_general(left, right, (((1,), (1,)), ((), ())), preferred_element_type=F32)


def lane_sum(value):
    return jnp.sum(value, axis=-1, keepdims=True)


def row_sum(value):
    return jnp.sum(value, axis=0, keepdims=True)


def when_equal(left, right, value=1.0):
    return jnp.where(left == right, value, 0.0)


def iota(shape, axis):
    return lax.broadcasted_iota(jnp.int32, shape, axis).astype(F32)


def whole_part(value, unit):
    return jnp.floor((value + 0.5) * (1.0 / unit))


def inverse_rms(value):
    return lax.rsqrt(jnp.mean(value * value, axis=-1, keepdims=True) + EPSILON)


def norm(value, gain):
    return value * inverse_rms(value) * gain


def norm_back(value, gain, grad):
    scale = inverse_rms(value)
    unit = value * scale
    scaled = grad * gain
    grad_value = scale * (scaled - unit * jnp.mean(scaled * unit, axis=-1, keepdims=True))
    return grad_value, row_sum(grad * unit)


def gelu_and_slope(hidden):
    rate = math.sqrt(2.0 / math.pi)
    square = hidden * hidden
    bend = jnp.tanh(hidden * (rate + rate * 0.044715 * square))
    share = 0.5 + 0.5 * bend
    act = hidden * share
    slope = share + act * (1.0 - bend) * (rate + 3.0 * rate * 0.044715 * square)
    return act, slope


class Sizes:
    def __init__(self, inputs, w_qkv, w_cross, w_router, w_up, table, experts):
        _, self.micro, self.tok, self.model = inputs.shape
        self.hidden = w_up.shape[-1]
        self.experts = experts
        self.tasks = table.shape[1]
        self.slots = 2 * self.tok
        self.halves = 2
        self.group = experts // self.halves
        self.bound = max(2, 6 * self.tok // experts)
        self.send = round_up(self.bound, 16)
        self.merged = self.halves * self.bound <= self.send
        self.flights = 1 if self.merged else self.halves
        self.half_rows = self.group * self.send
        self.all_rows = self.flights * self.half_rows
        self.misc = round_up(w_router.shape[-1] + 3, LANES)
        self.qkv_blocks = w_qkv.shape[-1] // LANES
        self.out_blocks = self.model // LANES
        self.cross_blocks = w_cross.shape[-1] // LANES
        self.misc_blocks = self.misc // LANES
        self.blocks = self.qkv_blocks + self.out_blocks + self.cross_blocks + self.misc_blocks
        self.bits = experts.bit_length() - 1
        unit = 16 * experts
        self.groups = []
        start = 0
        for blocks, count in (
            (self.cross_blocks, 3),
            (self.out_blocks, 2),
            (self.qkv_blocks + self.misc_blocks, 6),
        ):
            units = -(-blocks * self.model // unit)
            count = min(count, units)
            group = []
            for part in range(count):
                size = (units // count + (part < units % count)) * unit
                group.append((start, size))
                start += size
            self.groups.append(group)
        self.parts = sum(len(group) for group in self.groups)
        self.dense_rows = start


def kernel_body(z, names, *refs):
    r = SimpleNamespace(**dict(zip(names, refs)))
    me = lax.axis_index("expert")
    section = lax.axis_index("section")
    tok, model, micro, group, send, slots = (z.tok, z.model, z.micro, z.group, z.send, z.slots)
    here = lax.rem(me, group)
    base = me - here
    mirror = lax.rem(me + group, z.experts)
    me_f = me.astype(F32)
    here_f = here.astype(F32)
    base_f = base.astype(F32)
    enc_f = 1.0 - section.astype(F32)

    side = [None]
    owed = {}

    def on_section(index):
        def put(run):
            side[0] = index
            pl.when(section == index)(run)
            side[0] = None

        return put

    enc, dec = (on_section(0), on_section(1))

    def wait_for(ref, sem):
        pltpu.make_async_copy(ref, ref, sem).wait()

    def owe(key, copy):
        owed[side[0], key] = copy

    def settle(key):
        found = [e for e in owed if e[1] == key and (side[0] in (None, e[0]) or e[0] is None)]
        copies = [owed.pop(entry) for entry in found]
        if side[0] is not None and found[0][0] is None:
            owed[1 - side[0], key] = copies[0]
        wait_for(*copies[0]())

    def settle_all():
        for index in (None, 0, 1):
            waits = [owed.pop(entry) for entry in list(owed) if entry[0] == index]

            def run():
                for copy in waits:
                    wait_for(*copy())

            if index is None:
                run()
            else:
                pl.when(section == index)(run)

    loads = [
        pltpu.make_async_copy(source, target, r.load_sem.at[i])
        for i, (source, target) in enumerate(
            (
                (r.w_qkv, r.wqkv),
                (r.w_out, r.wout),
                (r.w_cross, r.wcross),
                (r.w_up, r.wup),
                (r.w_down, r.wdown),
            )
        )
    ]
    for load in loads:
        load.start()

    barrier = pltpu.get_barrier_semaphore()

    def greet(step, _):
        pl.semaphore_signal(
            barrier,
            inc=1,
            device_id={"expert": lax.rem(me + step, z.experts)},
            device_id_type=MESH,
        )
        return 0

    lax.fori_loop(1, z.experts, greet, 0)
    pl.semaphore_signal(
        barrier, inc=1, device_id={"section": 1 - section}, device_id_type=MESH
    )

    seg_rows = r.segments[...].astype(F32)
    task_rows = r.tasks[...].astype(F32)
    blank = jnp.zeros((LANES - 2 * micro, LANES), F32)
    flipped = jnp.transpose(jnp.concatenate([seg_rows, task_rows, blank], axis=0))
    lane = iota((1, LANES), 1)
    earlier = jnp.where(iota((tok, tok), 0) < iota((tok, tok), 1), 1.0, 0.0)
    ranks, counts = ([], [])
    for m in range(micro):
        task_col = flipped[:, micro + m : micro + m + 1]
        ranks.append(row_sum(when_equal(task_col, task_rows[m : m + 1]) * earlier))
        counts.append(row_sum(when_equal(task_col, lane)))
    r.infos[0] = jnp.concatenate(
        [task_rows, *ranks, *counts, jnp.zeros((8 - 3 * micro, LANES), F32)], axis=0
    )

    table = r.table[...].astype(F32)
    table_lane = iota((1, z.tasks), 1)

    def task_of(expert):
        return lane_sum(
            when_equal(table[0:1], expert, table_lane) + when_equal(table[1:2], expert, table_lane)
        )

    line = iota((z.half_rows, 1), 0)
    line_block = whole_part(line, send)
    line_rank = line - line_block * send
    line_place = here_f + line_block
    line_place = jnp.where(line_place >= group, line_place - group, line_place)
    line_task = task_of(base_f + line_place)

    def fill_pick(half):
        rank_here = line_rank - (half * z.bound if z.merged else 0)
        info = r.infos[half * group]
        for m in range(micro):
            hit = (info[INFO_TASK + m : INFO_TASK + m + 1] == line_task) & (
                info[INFO_RANK + m : INFO_RANK + m + 1] == rank_here
            )
            r.pick[half, m] = jnp.where(hit, 1.0, 0.0).astype(BF16)

    fill_pick(0)

    pl.semaphore_wait(barrier, z.experts)

    def tell(step, _):
        pltpu.make_async_remote_copy(
            src_ref=r.infos.at[0],
            dst_ref=r.infos.at[step],
            send_sem=r.info_send,
            recv_sem=r.info_recv,
            device_id={"expert": lax.rem(me + step, z.experts)},
            device_id_type=MESH,
        ).start()
        return 0

    lax.fori_loop(1, z.experts, tell, 0)
    others_told = pl.ds(1, z.experts - 1)
    owe(SENT, lambda: (r.infos.at[others_told], r.info_send))
    owe(0, lambda: (r.infos.at[others_told], r.info_recv))

    def spread(way, m, half, rows, back):
        packed, landed = (
            (r.reply_out, r.reply_in) if back else (r.rows_out, r.rows_in)
        )
        send_sem, recv_sem = (
            (r.reply_send, r.reply_recv) if back else (r.rows_send, r.rows_recv)
        )
        packed[way, m, half] = rows.reshape(group, send, model)
        landed[way, m, half, 0] = rows[:send]

        def push(step, _):
            if back:
                other = lax.rem(here + group - step, group)
            else:
                other = lax.rem(here + step, group)
            pltpu.make_async_remote_copy(
                src_ref=packed.at[way, m, half, step],
                dst_ref=landed.at[way, m, half, step],
                send_sem=send_sem.at[way, m, half],
                recv_sem=recv_sem.at[way, m, half],
                device_id={"expert": base + other},
                device_id_type=MESH,
            ).start()
            return 0

        lax.fori_loop(1, group, push, 0, unroll=group <= 8)
        key = (REPLY if back else ROWS) + 100 * way + 10 * m + half
        others = pl.ds(1, group - 1)
        at = (way, m, half)
        owe(SENT + key, lambda: (packed.at[(*at, others)], send_sem.at[at]))
        owe(key, lambda: (landed.at[(*at, others)], recv_sem.at[at]))

    def ship(key, source, target, sems, device_id):
        copy = pltpu.make_async_remote_copy(
            src_ref=source(),
            dst_ref=target(),
            send_sem=sems()[0],
            recv_sem=sems()[1],
            device_id=device_id,
            device_id_type=MESH,
        )
        copy.start()
        owe(SENT + key, lambda: (source(), sems()[0]))

    def swap(key, source, target, sems):
        ship(key, source, target, sems, {"expert": mirror})
        owe(key, lambda: (target(), sems()[1]))

    def dispatch(way, m, source):
        swap(
            MIRROR + 10 * way + m,
            lambda: source.at[m],
            lambda: r.mirror_rows.at[way, m],
            lambda: (r.mirror_send.at[way, m], r.mirror_recv.at[way, m]),
        )
        if not z.merged:
            spread(way, m, 0, dot(r.pick[0, m], source[m]).astype(BF16), False)

    def dispatch_mirror(way, m, source):
        settle(MIRROR + 10 * way + m)
        rows = dot(r.pick[1, m], r.mirror_rows[way, m])
        if z.merged:
            rows += dot(r.pick[0, m], source[m])
        spread(way, m, z.flights - 1, rows.astype(BF16), False)

    def arrived(way, m):
        for half in range(z.flights):
            settle(ROWS + 100 * way + 10 * m + half)
        return dot(r.compact[m], r.rows_in[way, m].reshape(z.all_rows, model))

    def combine(way, m, rows):
        reply = dot_rows(r.compact[m], rows).astype(BF16)
        for half in reversed(range(z.flights)):
            spread(way, m, half, reply[half * z.half_rows : (half + 1) * z.half_rows], True)

    def gathered(way, m, half):
        flight = 0 if z.merged else half
        if not z.merged or half == 1:
            settle(REPLY + 100 * way + 10 * m + flight)
        return dot_rows(r.pick[half, m], r.reply_in[way, m, flight].reshape(z.half_rows, model))

    def combine_mirror(way, m):
        r.sums_out[way, m] = gathered(way, m, 1).astype(BF16)
        swap(
            SUMS + 10 * way + m,
            lambda: r.sums_out.at[way, m],
            lambda: r.sums_in.at[way, m],
            lambda: (r.sums_send.at[way, m], r.sums_recv.at[way, m]),
        )

    def combine_end(way, m):
        own = gathered(way, m, 0)
        settle(SUMS + 10 * way + m)
        return own + r.sums_in[way, m].astype(F32)

    def know_others():
        settle(0)
        fill_pick(1)

    @dec
    def _():
        dispatch(1, 0, r.cotangent)
        know_others()
        dispatch_mirror(1, 0, r.cotangent)

    low_lane = jnp.where(iota((1, LANES), 1) < LANES // 2, 1.0, 0.0)
    high_lane = 1.0 - low_lane
    low_bf, high_bf = (low_lane.astype(BF16), high_lane.astype(BF16))
    pairs = model // LANES
    score_scale = (model // HEADS) ** (-0.5)

    def stacked(block):
        return jnp.concatenate([block * low_bf, block * high_bf], axis=0)

    def merged(block):
        return block[:tok] * low_lane + block[tok:] * high_lane

    def attend(queries, keys, values, allowed):
        scores = dot_cols(stacked(queries), keys) * score_scale
        if allowed is not None:
            scores = jnp.where(allowed > 0.5, scores, -1000000000.0)
        top = jnp.max(scores, axis=-1, keepdims=True)
        grown = jnp.exp(scores - top)
        probs = grown / lane_sum(grown)
        return probs, merged(dot(probs.astype(BF16), values))

    def attend_back(queries, keys, values, probs, grad_mixed):
        grad_stack = stacked(grad_mixed)
        grad_probs = dot_cols(grad_stack, values)
        inner = lane_sum(probs * grad_probs)
        grad_scores = (probs * (grad_probs - inner)).astype(BF16)
        grad_queries = merged(dot(grad_scores, keys)) * score_scale
        grad_keys = dot_rows(grad_scores, stacked(queries)) * score_scale
        grad_values = dot_rows(probs.astype(BF16), grad_stack)
        return grad_queries, grad_keys, grad_values

    def cols(index, start=0):
        return pl.ds(pl.multiple_of(start + index * LANES, LANES), LANES)

    def each_pair(run):
        def step(pair, _):
            run(pair)
            return 0

        lax.fori_loop(0, pairs, step, 0, unroll=UNROLL)

    gain_a, gain_c, gain_m = [r.gains[:, i * model : (i + 1) * model] for i in range(3)]

    def enter_experts(m):
        r.normed_m[m] = norm(r.after_cross[m], gain_m).astype(BF16)
        dispatch(0, m, r.normed_m)

    loads[0].wait()
    loads[1].wait()
    for m in range(micro):
        x_in = r.inputs[m].astype(F32)
        normed_a = norm(x_in, gain_a).astype(BF16)
        r.normed_a[m] = normed_a
        r.qkv[m] = dot(normed_a, r.wqkv[...]).astype(BF16)
        causal = jnp.where(iota((tok, tok), 1) <= iota((tok, tok), 0), 1.0, enc_f)
        allowed = when_equal(flipped[:, m : m + 1], seg_rows[m : m + 1]) * causal
        allowed = jnp.concatenate([allowed, allowed], axis=0)
        @each_pair
        def _(pair):
            probs, mixed = attend(
                r.qkv[m, :, cols(pair)],
                r.qkv[m, :, cols(pair, model)],
                r.qkv[m, :, cols(pair, 2 * model)],
                allowed,
            )
            r.probs_self[m, pair] = probs
            r.attn_rows[m, :, cols(pair)] = mixed.astype(BF16)
        after_self = x_in + dot(r.attn_rows[m], r.wout[...])

        @enc
        def _():
            r.after_cross[m] = after_self
            enter_experts(m)

        @dec
        def _():
            r.after_self[m] = after_self

    loads[2].wait()

    def send_memory(m):
        index = m + micro * side[0]
        ship(
            MEMORY + index,
            lambda: r.memory_out.at[m],
            lambda: r.memory.at[m],
            lambda: (r.memory_send.at[index], r.memory_recv.at[index]),
            {"section": 1 - section},
        )

    def wait_memory(m):
        index = m + micro * (1 - side[0])
        owe(MEMORY + index, lambda: (r.memory.at[m], r.memory_recv.at[index]))
        settle(MEMORY + index)

    @enc
    def _():
        know_others()

    @dec
    def _():
        for m in range(micro):
            after_self = r.after_self[m]
            normed_c = norm(after_self, gain_c).astype(BF16)
            r.normed_c[m] = normed_c
            r.cross_q[m] = dot(normed_c, r.wcross[:, :model]).astype(BF16)
            wait_memory(m)

            @each_pair
            def _(pair):
                probs, mixed = attend(
                    r.cross_q[m, :, cols(pair)],
                    r.memory[m, :, cols(pair)],
                    r.memory[m, :, cols(pair, model)],
                    None,
                )
                r.probs_cross[m, pair] = probs
                r.cross_rows[m, :, cols(pair)] = mixed.astype(BF16)

            r.after_cross[m] = after_self + dot_cols(r.cross_rows[m], r.wcross[:, model:])
            enter_experts(m)

    for m in range(micro):
        dispatch_mirror(0, m, r.normed_m)

    @dec
    def _():
        for m in range(1, micro):
            dispatch(1, m, r.cotangent)
        for m in range(1, micro):
            dispatch_mirror(1, m, r.cotangent)

    own_task = task_of(me_f)
    partner = lane_sum(when_equal(table_lane, own_task, table[0:1] + table[1:2])) - me_f
    capacity = r.capacity[0].astype(F32)
    place = iota((1, z.all_rows), 1)
    block = whole_part(place, send)
    place_rank = place - block * send
    place_half = whole_part(block, group)
    sender = here_f - (block - place_half * group)
    if z.merged:
        place_half = jnp.minimum(whole_part(place_rank, z.bound), 1.0)
        place_rank = place_rank - place_half * z.bound
    sender = base_f + jnp.where(sender < 0.0, sender + group, sender) + place_half * group
    sender = jnp.where(sender >= z.experts, sender - z.experts, sender)
    teller = me_f - iota((z.experts, 1), 0)
    teller = jnp.where(teller < 0.0, teller + z.experts, teller)
    for m in range(micro):
        told = lane_sum(jnp.where(lane == own_task, r.infos[:, INFO_COUNT + m, :], 0.0))
        count = row_sum(when_equal(teller, sender, told))
        slot = row_sum(jnp.where(teller < sender, told, 0.0)) + place_rank
        slot = jnp.where((place_rank < count) & (slot < capacity), slot, -1.0)
        r.compact[m] = when_equal(iota((slots, 1), 0), slot).astype(BF16)

    router = r.w_router[...]
    routers = router.shape[0]
    expert_lane = iota((8, routers), 1)
    sign = when_equal(expert_lane, me_f) - when_equal(expert_lane, partner)
    router_step = dot(sign.astype(BF16), router)[0:1]
    tile = 1024

    def each_tile(width, run):
        def step(index, _):
            run(pl.ds(pl.multiple_of(index * tile, tile), tile))
            return 0

        lax.fori_loop(0, width // tile, step, 0)

    def expert_forward(m):
        taken = arrived(0, m).astype(BF16)
        r.taken[m] = taken

        def up_tile(at):
            act, slope = gelu_and_slope(dot(r.taken[m], r.wup[:, at]))
            r.act[m, :, at] = act.astype(BF16)
            r.slope[m, :, at] = slope.astype(BF16)

        each_tile(z.hidden, up_tile)
        gap = lane_sum(taken.astype(F32) * router_step)
        small = jnp.exp(-jnp.abs(gap))
        large = 1.0 / (1.0 + small)
        gate = jnp.where(gap >= 0.0, large, small * large)
        r.gate[m] = gate
        r.gate_slope[m] = small * large * large

        r.expert_out[m] = dot(r.act[m], r.wdown[...]).astype(BF16)
        r.gated[m] = (gate * r.expert_out[m].astype(F32)).astype(BF16)

    def expert_backward(m):
        grad_final = arrived(1, m)
        grad_gate = lane_sum(r.expert_out[m].astype(F32) * grad_final)
        grad_gap = r.gate_slope[m] * grad_gate
        r.grad_gap[m] = grad_gap
        r.grad_out[m] = (r.gate[m] * grad_final).astype(BF16)

        def act_tile(at):
            grad_act = dot_cols(r.grad_out[m], r.wdown[at, :])
            r.grad_hidden[m, :, at] = (grad_act * r.slope[m, :, at].astype(F32)).astype(BF16)

        each_tile(z.hidden, act_tile)

        rounded = dot_cols(r.grad_hidden[m], r.wup[...]).astype(BF16).astype(F32)
        combine(1, m, (rounded + grad_gap * router_step).astype(BF16))

    loads[3].wait()
    loads[4].wait()

    @dec
    def _():
        for m in range(micro):
            expert_forward(m)
            expert_backward(m)
        for m in range(micro):
            r.grad_state[m] = r.cotangent[m].astype(F32)

    @enc
    def _():
        for m in range(micro):
            expert_forward(m)
            combine(0, m, r.gated[m])
        for m in range(micro):
            combine_mirror(0, m)
        for m in range(micro):
            layer_final = r.after_cross[m] + combine_end(0, m)
            r.layer_final[m] = layer_final
            r.layer_out[m] = layer_final.astype(BF16)
            normed_k = norm(layer_final, gain_c).astype(BF16)
            r.normed_c[m] = normed_k
            r.memory_out[m] = dot(normed_k, r.wcross[...]).astype(BF16)
            send_memory(m)
        gain_grad = jnp.zeros((1, model), F32)
        for m in range(micro):
            wait_memory(m)
            grad_normed = dot_cols(r.memory[m], r.wcross[...])
            grad_state, grad_gain = norm_back(r.layer_final[m], gain_c, grad_normed)
            gain_grad += grad_gain
            grad_final = r.cotangent[m].astype(F32) + grad_state
            r.grad_state[m] = grad_final
            r.grad_rows[m] = grad_final.astype(BF16)
            dispatch(1, m, r.grad_rows)
        for m in range(micro):
            dispatch_mirror(1, m, r.grad_rows)
        r.gain_grads[1:2] = gain_grad
        for m in range(micro):
            expert_backward(m)

    def flat(ref, at=slice(None)):
        value = ref[:, :, at]
        return value.reshape(value.shape[0] * value.shape[1], value.shape[2])

    saves = []

    def save(source, target):
        copy = pltpu.make_async_copy(source, target, r.save_sem.at[len(saves)])
        copy.start()
        saves.append(copy)

    def up_grad(at):
        r.wup[:, at] = dot_rows(flat(r.taken), flat(r.grad_hidden, at)).astype(BF16)

    def down_grad(at):
        r.wdown[at, :] = dot_rows(flat(r.act, at), flat(r.grad_out)).astype(BF16)

    each_tile(z.hidden, up_grad)
    save(r.wup, r.up_grad)
    for m in range(micro):
        combine_mirror(1, m)
    each_tile(z.hidden, down_grad)
    save(r.wdown, r.down_grad)

    gain_grad = jnp.zeros((1, model), F32)
    for m in range(micro):
        grad_state, grad_gain = norm_back(r.after_cross[m], gain_m, combine_end(1, m))
        gain_grad += grad_gain
        r.grad_state[m] += grad_state

        @dec
        def _():
            grad_y = r.grad_state[m].astype(BF16)
            r.grad_cross[m] = grad_y
            r.grad_mix[...] = dot(grad_y, r.wcross[:, model:]).astype(BF16)

            @each_pair
            def _(pair):
                at = cols(pair)
                grad_q, grad_k, grad_v = attend_back(
                    r.cross_q[m, :, at],
                    r.memory[m, :, at],
                    r.memory[m, :, cols(pair, model)],
                    r.probs_cross[m, pair],
                    r.grad_mix[:, at],
                )
                r.grad_cross_q[m, :, at] = grad_q.astype(BF16)
                r.memory_out[m, :, at] = grad_k.astype(BF16)
                r.memory_out[m, :, cols(pair, model)] = grad_v.astype(BF16)
            send_memory(m)

    r.gain_grads[2:3] = gain_grad

    @dec
    def _():
        gain_grad = jnp.zeros((1, model), F32)
        for m in range(micro):
            grad_normed = dot_cols(r.grad_cross_q[m], r.wcross[:, :model])
            grad_state, grad_gain = norm_back(r.after_self[m], gain_c, grad_normed)
            gain_grad += grad_gain
            r.grad_state[m] += grad_state
        r.gain_grads[1:2] = gain_grad
        for m in range(micro):
            combine(0, m, r.gated[m])

    first_cross = 0
    first_out = first_cross + z.cross_blocks
    first_qkv = first_out + z.out_blocks
    first_misc = first_qkv + z.qkv_blocks

    def store_blocks(first, left, right):
        width = 2 * LANES
        left = flat(left)
        for start in range(0, right.shape[-1], width):
            grad = dot_rows(left, flat(right, pl.ds(start, width))).astype(BF16)
            at = (first + start // LANES) * model
            r.dense[at : at + model] = grad[:, :LANES]
            r.dense[at + model : at + 2 * model] = grad[:, LANES:]

    bits = list(range(z.bits))
    lead = min(3, z.bits)
    parts = []
    for group_index, group_parts in enumerate(z.groups):
        for start, size in group_parts:
            turn = len(parts) % lead
            parts.append(
                SimpleNamespace(
                    index=len(parts),
                    group=group_index,
                    order=bits[turn:lead] + bits[:turn] + bits[lead:],
                    at=jnp.int32(start),
                    size=size,
                    land=start,
                    stage=0,
                    copy=None,
                )
            )

    def aligned(start, size):
        return pl.ds(pl.multiple_of(start, 16), size)

    def start_stage(part):
        halving = part.stage < z.bits
        stride = 1 << part.order[part.stage if halving else 2 * z.bits - 1 - part.stage]
        part.bit = lax.rem(lax.div(me, stride), 2)
        if halving:
            half = part.size // 2
            source = r.dense.at[aligned(part.at + (1 - part.bit) * half, half)]
            target = r.partial.at[pl.ds(part.land, half)]
        else:
            source = target = r.total.at[aligned(part.at, part.size)]
        part.copy = pltpu.make_async_remote_copy(
            src_ref=source,
            dst_ref=target,
            send_sem=r.sum_send.at[part.index, part.stage],
            recv_sem=r.sum_recv.at[part.index, part.stage],
            device_id={"expert": me + (1 - 2 * part.bit) * stride},
            device_id_type=MESH,
        )
        part.copy.start()

    def end_stage(part):
        part.copy.wait()
        if part.stage < z.bits:
            half = part.size // 2
            part.at = part.at + part.bit * half
            rows = aligned(part.at, half)
            came = r.partial[pl.ds(part.land, half)].astype(F32)
            target = r.total if part.stage == z.bits - 1 else r.dense
            target[rows] = (r.dense[rows].astype(F32) + came).astype(BF16)
            part.land += half
            part.size = half
        else:
            part.at = part.at - part.bit * part.size
            part.size *= 2
        part.stage += 1

    def begin(group_index):
        for part in parts:
            if part.group == group_index:
                start_stage(part)

    def advance(group_index):
        for part in parts:
            if part.group == group_index and part.stage < 2 * z.bits:
                end_stage(part)
                if part.stage < 2 * z.bits:
                    start_stage(part)

    @enc
    def _():
        store_blocks(first_cross, r.normed_c, r.memory)

    @dec
    def _():
        store_blocks(first_cross, r.normed_c, r.grad_cross_q)
        store_blocks(first_cross + z.out_blocks, r.grad_cross, r.cross_rows)

    begin(0)
    for m in range(micro):
        r.grad_self[m] = r.grad_state[m].astype(BF16)
    store_blocks(first_out, r.attn_rows, r.grad_self)
    begin(1)

    gain_grad = jnp.zeros((1, model), F32)
    for m in range(micro):
        grad_top = r.grad_state[m]
        grad_y = r.grad_self[m]
        r.grad_mix[...] = dot_cols(grad_y, r.wout[...]).astype(BF16)

        @each_pair
        def _(pair):
            grads = attend_back(
                r.qkv[m, :, cols(pair)],
                r.qkv[m, :, cols(pair, model)],
                r.qkv[m, :, cols(pair, 2 * model)],
                r.probs_self[m, pair],
                r.grad_mix[:, cols(pair)],
            )
            for third, grad in enumerate(grads):
                r.grad_qkv[m, :, cols(pair, third * model)] = grad.astype(BF16)
        grad_normed = dot_cols(r.grad_qkv[m], r.wqkv[...])
        grad_state, grad_gain = norm_back(r.inputs[m].astype(F32), gain_a, grad_normed)
        gain_grad += grad_gain
        r.inputs_grad[m] = grad_top + grad_state
    r.gain_grads[0:1] = gain_grad
    r.gain_grads[3:8] = jnp.zeros((5, model), F32)

    store_blocks(first_qkv, r.normed_a, r.grad_qkv)
    misc_row = iota((1, z.misc), 1)
    misc_sign = when_equal(misc_row, me_f) - when_equal(misc_row, partner)
    misc = jnp.zeros((z.misc, model), F32)
    for m in range(micro):
        steps = r.grad_gap[m] * misc_sign
        top = steps.astype(BF16)
        rest = (steps - top.astype(F32)).astype(BF16)
        misc += dot_rows(top, r.taken[m]) + dot_rows(rest, r.taken[m])
    place_gain = when_equal(iota((8, z.misc), 1), iota((8, z.misc), 0) + routers)
    misc += dot_rows(place_gain.astype(BF16), r.gain_grads[...].astype(BF16))
    misc_rows = [
        pl.ds(first_misc * model + index * z.misc, z.misc) for index in range(model // LANES)
    ]
    for index, rows in enumerate(misc_rows):
        r.dense[rows] = misc[:, index * LANES : (index + 1) * LANES].astype(BF16)
    used = z.blocks * model
    if used < z.dense_rows:
        r.dense[used:] = jnp.zeros((z.dense_rows - used, LANES), BF16)
    begin(2)
    advance(0)
    advance(1)

    @dec
    def _():
        for m in range(micro):
            combine_mirror(0, m)
        for m in range(micro):
            r.layer_out[m] = (r.after_cross[m] + combine_end(0, m)).astype(BF16)

    while any(part.stage < 2 * z.bits for part in parts):
        for group_index in range(3):
            advance(group_index)

    for target, first, count in (
        (r.cross_grad, first_cross, z.cross_blocks),
        (r.out_grad, first_out, z.out_blocks),
        (r.qkv_grad, first_qkv, z.qkv_blocks),
    ):
        for index in range(count):
            rows = pl.ds((first + index) * model, model)
            save(r.total.at[rows], target.at[:, pl.ds(index * LANES, LANES)])
    for index, rows in enumerate(misc_rows):
        sums = r.total[rows].astype(F32)
        r.router_grad[:, index * LANES : (index + 1) * LANES] = sums[:routers]
        for row in range(3):
            at = row * model + index * LANES
            r.gains_grad[:, at : at + LANES] = sums[routers + row : routers + row + 1]
    for copy in saves:
        copy.wait()

    settle_all()


def vmem_bytes(buffers):
    total = 0
    for buffer in buffers:
        if buffer.memory_space == pltpu.VMEM:
            *lead, rows, lanes = buffer.shape
            size = math.prod(lead) * round_up(rows, 8) * round_up(lanes, LANES)
            total += size * jnp.dtype(buffer.dtype).itemsize
    return min(total + 5 * 1024 * 1024, 62 * 1024 * 1024)


def run_kernel(z, arrays):
    micro, tok, model, hidden = (z.micro, z.tok, z.model, z.hidden)
    vmem = pl.BlockSpec(memory_space=pltpu.VMEM)
    hbm = pl.BlockSpec(memory_space=pl.ANY)
    inputs = dict(
        segments=(arrays.segments, vmem),
        tasks=(arrays.tasks, vmem),
        table=(arrays.table, vmem),
        capacity=(arrays.capacity, pl.BlockSpec(memory_space=pltpu.SMEM)),
        inputs=(arrays.inputs, vmem),
        cotangent=(arrays.cotangent, vmem),
        gains=(arrays.gains, vmem),
        w_router=(arrays.w_router, vmem),
        w_qkv=(arrays.w_qkv, hbm),
        w_out=(arrays.w_out, hbm),
        w_cross=(arrays.w_cross, hbm),
        w_up=(arrays.w_up, hbm),
        w_down=(arrays.w_down, hbm),
    )
    rows = (micro, tok, model)
    slot_rows = (micro, z.slots, model)
    slot_hidden = (micro, z.slots, hidden)
    outputs = dict(
        layer_out=(rows, BF16, vmem),
        inputs_grad=(rows, F32, vmem),
        gains_grad=((1, 3 * model), F32, vmem),
        router_grad=(arrays.w_router.shape, F32, vmem),
        qkv_grad=(arrays.w_qkv.shape, BF16, hbm),
        out_grad=(arrays.w_out.shape, BF16, hbm),
        cross_grad=(arrays.w_cross.shape, BF16, hbm),
        up_grad=(arrays.w_up.shape, BF16, hbm),
        down_grad=(arrays.w_down.shape, BF16, hbm),
    )
    blocks = (2, micro, z.flights, z.group, z.send, model)
    pairs = model // LANES
    dma = pltpu.SemaphoreType.DMA
    scratch = dict(
        wqkv=pltpu.VMEM(arrays.w_qkv.shape, BF16),
        wout=pltpu.VMEM(arrays.w_out.shape, BF16),
        wcross=pltpu.VMEM(arrays.w_cross.shape, BF16),
        wup=pltpu.VMEM(arrays.w_up.shape, BF16),
        wdown=pltpu.VMEM(arrays.w_down.shape, BF16),
        infos=pltpu.VMEM((z.experts, 8, LANES), F32),
        normed_a=pltpu.VMEM(rows, BF16),
        qkv=pltpu.VMEM((micro, tok, 3 * model), BF16),
        probs_self=pltpu.VMEM((micro, pairs, 2 * tok, tok), F32),
        attn_rows=pltpu.VMEM(rows, BF16),
        after_self=pltpu.VMEM(rows, F32),
        normed_c=pltpu.VMEM(rows, BF16),
        cross_q=pltpu.VMEM(rows, BF16),
        probs_cross=pltpu.VMEM((micro, pairs, 2 * tok, tok), F32),
        cross_rows=pltpu.VMEM(rows, BF16),
        memory_out=pltpu.VMEM((micro, tok, 2 * model), BF16),
        memory=pltpu.VMEM((micro, tok, 2 * model), BF16),
        after_cross=pltpu.VMEM(rows, F32),
        normed_m=pltpu.VMEM(rows, BF16),
        layer_final=pltpu.VMEM(rows, F32),
        grad_state=pltpu.VMEM(rows, F32),
        grad_rows=pltpu.VMEM(rows, BF16),
        grad_cross=pltpu.VMEM(rows, BF16),
        grad_cross_q=pltpu.VMEM(rows, BF16),
        grad_self=pltpu.VMEM(rows, BF16),
        grad_mix=pltpu.VMEM((tok, model), BF16),
        grad_qkv=pltpu.VMEM((micro, tok, 3 * model), BF16),
        gain_grads=pltpu.VMEM((8, model), F32),
        pick=pltpu.VMEM((z.halves, micro, z.half_rows, tok), BF16),
        compact=pltpu.VMEM((micro, z.slots, z.all_rows), BF16),
        rows_out=pltpu.VMEM(blocks, BF16),
        rows_in=pltpu.VMEM(blocks, BF16),
        reply_out=pltpu.VMEM(blocks, BF16),
        reply_in=pltpu.VMEM(blocks, BF16),
        mirror_rows=pltpu.VMEM((2,) + rows, BF16),
        sums_out=pltpu.VMEM((2,) + rows, BF16),
        sums_in=pltpu.VMEM((2,) + rows, BF16),
        taken=pltpu.VMEM(slot_rows, BF16),
        slope=pltpu.VMEM(slot_hidden, BF16),
        act=pltpu.VMEM(slot_hidden, BF16),
        expert_out=pltpu.VMEM(slot_rows, BF16),
        gated=pltpu.VMEM(slot_rows, BF16),
        gate=pltpu.VMEM((micro, z.slots, 1), F32),
        gate_slope=pltpu.VMEM((micro, z.slots, 1), F32),
        grad_gap=pltpu.VMEM((micro, z.slots, 1), F32),
        grad_out=pltpu.VMEM(slot_rows, BF16),
        grad_hidden=pltpu.VMEM(slot_hidden, BF16),
        dense=pltpu.VMEM((z.dense_rows, LANES), BF16),
        total=pltpu.VMEM((z.dense_rows, LANES), BF16),
        partial=pltpu.VMEM((z.dense_rows, LANES), BF16),
        load_sem=dma((5,)),
        save_sem=dma((2 + z.blocks - z.misc_blocks,)),
        info_send=dma(()),
        info_recv=dma(()),
        rows_send=dma((2, micro, z.flights)),
        rows_recv=dma((2, micro, z.flights)),
        reply_send=dma((2, micro, z.flights)),
        reply_recv=dma((2, micro, z.flights)),
        mirror_send=dma((2, micro)),
        mirror_recv=dma((2, micro)),
        sums_send=dma((2, micro)),
        sums_recv=dma((2, micro)),
        memory_send=dma((2 * micro,)),
        memory_recv=dma((2 * micro,)),
        sum_send=dma((z.parts, 2 * z.bits)),
        sum_recv=dma((z.parts, 2 * z.bits)),
    )
    names = [*inputs, *outputs, *scratch]

    def body(*refs):
        kernel_body(z, names, *refs)

    return pl.pallas_call(
        body,
        name="layer_step",
        out_shape=[jax.ShapeDtypeStruct(shape, dtype) for shape, dtype, _ in outputs.values()],
        in_specs=[spec for _, spec in inputs.values()],
        out_specs=[spec for _, _, spec in outputs.values()],
        scratch_shapes=list(scratch.values()),
        compiler_params=pltpu.CompilerParams(
            collective_id=0, has_side_effects=True, vmem_limit_bytes=vmem_bytes(scratch.values())
        ),
    )(*[value for value, _ in inputs.values()])


def shards(
    inputs,
    cotangent,
    segments,
    tasks,
    table,
    capacity,
    gains,
    w_qkv,
    w_out,
    w_cross,
    w_router,
    w_up,
    w_down,
):
    experts = lax.axis_size("expert")
    z = Sizes(inputs, w_qkv, w_cross, w_router, w_up, table, experts)
    model = z.model
    arrays = SimpleNamespace(
        segments=segments[0],
        tasks=tasks[0, :, :, 0],
        table=table[0].T,
        capacity=capacity,
        inputs=inputs[0],
        cotangent=cotangent[0],
        gains=gains.reshape(1, 3 * model),
        w_router=w_router[0].T,
        w_qkv=w_qkv[0],
        w_out=w_out[0],
        w_cross=w_cross[0],
        w_up=w_up[0, 0],
        w_down=w_down[0, 0],
    )
    out, inputs_grad, gains_grad, router_grad, *grads = run_kernel(z, arrays)
    qkv_grad, out_grad, cross_grad, up_grad, down_grad = [grad.astype(F32) for grad in grads]
    return (
        out[None],
        inputs_grad[None],
        gains_grad.reshape(1, 3, model),
        qkv_grad[None],
        out_grad[None],
        cross_grad[None],
        router_grad.T[None],
        up_grad[None, None],
        down_grad[None, None],
    )


def solution(mesh):
    in_specs = (
        P("section", None, "expert", None),
        P("section", None, "expert", None),
        P("section", None, "expert"),
        P("section", None, "expert", None),
        P("section", None, None),
        P("section"),
        P("section", None, None),
        P("section", None, None),
        P("section", None, None),
        P("section", None, None),
        P("section", None, None),
        P("section", "expert", None, None),
        P("section", "expert", None, None),
    )
    out_specs = (
        P("section", None, "expert", None),
        P("section", None, "expert", None),
        P("section", None, None),
        P("section", None, None),
        P("section", None, None),
        P("section", None, None),
        P("section", None, None),
        P("section", "expert", None, None),
        P("section", "expert", None, None),
    )
    return jax.shard_map(shards, mesh=mesh, in_specs=in_specs, out_specs=out_specs, check_vma=False)
```

time: 234 us -> 200 us (0.85)
  local copies, waits for them, and re-layouts: 21.9 us -> 2.73 us
  Pallas kernels: 201 us -> 184 us
  other arithmetic: 1.13 us -> 11.6 us
  matrix products: 8.51 us -> 0 us
    pallas_call x1, Pallas kernels: 201 us -> 184 us  [run_kernel(): pl.pallas_call(body, name='layer_step', out_shape=[jax.ShapeDtypeStruct(s...]
    broadcast_in_dim x0 -> x5, other arithmetic: none -> 11.6 us  [the longest x1 4.35 us: shards(): down_grad[None, None]]
    dot_general x2 -> x0, matrix products: 8.51 us -> none  [dot_rows(): lax.dot_general(left, right, (((0,), (0,)), ((), ())), preferred_element_...]
    convert_element_type x5 -> x0, local copies, waits for them, and re-layouts: 6.48 us -> none  [blocks_of(): return part.transpose(1, 0, 2).reshape(model, count * LANES).astype(F32)]
    unnamed x16 -> x20, local copies, waits for them, and re-layouts: 8.83 us -> 2.73 us
    slice x3 -> x0, local copies, waits for them, and re-layouts: 5.02 us -> none  [blocks_of(): dense[first * model:(first + count) * model].reshape(count, model, LANES)]
where the time goes in v2:
time: 200 us
  Pallas kernels  184 us (92%)
  other arithmetic  11.6 us (6%)
  local copies, waits for them, and re-layouts  2.73 us (1%)
    pallas_call x1, Pallas kernels, run_kernel(): pl.pallas_call(body, name='layer_step', out_shape=[jax.ShapeDtypeStruct(s...  184 us
    broadcast_in_dim x1, other arithmetic, shards(): down_grad[None, None]  4.35 us

profile of v2, /device:TPU:0, one launch (start us, length us, event | category | flops | bytes accessed | tf_op | source)
XLA Modules:
  0.0 199.9 jit_solution(14969811715987934524)
XLA Ops:
  1.3 184.2 %layer_step.1 = (bf16[2,128,512]{2,1,0:T(8,128)(2,1)}, f32[2,128,512]{2,1,0:T(8,128)}, f32[1,1536]{1,0:T(1,128)}, f32[16,512]{1,0:T(8,128)}, bf16[512,1536]{1,0:...) custom-call(s32[2,128]{1,0:T(2,128)} %bitcast.50, ...), custom_call_target="tpu_custom_call" | custom-call | tf_op jit(solution)/shard_map/layer_step/pallas_call | solution.py:981
  185.5 0.0 copy-start
  185.5 4.3 %bitcast_convert_fusion = f32[1,1,2048,512]{3,2,1,0:T(8,128)} fusion(bf16[2048,512]{1,0:T(8,128)(2,1)} %get-tuple-element.26), kind=kLoop, calls=%fused_computation | loop fusion | flops 1048576 | bytes 6291456 | tf_op jit(solution)/shard_map/broadcast_in_dim | solution.py:1038
  189.8 0.0 copy-done
  189.8 0.0 copy-start.1
  189.8 2.5 %bitcast_convert_fusion.1 = f32[1,1,512,2048]{3,2,1,0:T(8,128)} fusion(bf16[512,2048]{1,0:T(8,128)(2,1)S(1)} %copy-done), kind=kLoop, calls=%fused_computation.1 | loop fusion | flops 1048576 | bytes 6291456 | tf_op jit(solution)/shard_map/broadcast_in_dim | solution.py:1037
  192.4 0.0 copy-done.1
  192.4 0.0 copy-start.2
  192.4 2.1 %bitcast_convert_fusion.2 = f32[1,512,1536]{2,1,0:T(8,128)} fusion(bf16[512,1536]{1,0:T(8,128)(2,1)S(1)} %copy-done.1), kind=kLoop, calls=%fused_computation.2 | loop fusion | flops 786432 | bytes 4718592 | tf_op jit(solution)/shard_map/broadcast_in_dim | solution.py:1033
  194.4 0.0 copy-start.3
  194.4 0.0 copy-done.2
  194.4 0.0 copy-start.5
  194.5 0.0 copy-start.4
  194.5 1.6 bitcast_convert_fusion.3
  196.0 0.0 copy-start.7
  196.0 0.0 copy-start.6
  196.0 0.0 copy-done.3
  196.0 1.1 bitcast_convert_fusion.4
  197.1 0.0 copy-done.5
  197.1 0.7 copy.29
  197.8 0.0 copy-done.4
  197.8 0.8 copy.30
  198.6 0.0 copy-done.7
  198.6 0.6 copy.31
  199.2 0.0 copy-done.6
  199.2 0.6 copy.32
Async XLA Ops:
  185.5 4.4 %copy-start = (bf16[512,2048]{1,0:T(8,128)(2,1)S(1)}, bf16[512,2048]{1,0:T(8,128)(2,1)}, u32[]{:S(2)}) copy-start(bf16[512,2048]{1,0:T(8,128)(2,1)} %get-tuple-element.25) | copy-start | bytes 6291460
  189.8 2.5 %copy-start.1 = (bf16[512,1536]{1,0:T(8,128)(2,1)S(1)}, bf16[512,1536]{1,0:T(8,128)(2,1)}, u32[]{:S(2)}) copy-start(bf16[512,1536]{1,0:T(8,128)(2,1)} %get-tuple-element.21) | copy-start | bytes 4718596
  192.4 2.1 %copy-start.2 = (bf16[512,1024]{1,0:T(8,128)(2,1)S(1)}, bf16[512,1024]{1,0:T(8,128)(2,1)}, u32[]{:S(2)}) copy-start(bf16[512,1024]{1,0:T(8,128)(2,1)} %get-tuple-element.23) | copy-start | bytes 3145732
  194.4 1.6 copy-start.3
  194.4 2.7 %copy-start.5 = (bf16[2,128,512]{2,1,0:T(8,128)(2,1)S(1)}, bf16[2,128,512]{2,1,0:T(8,128)(2,1)}, u32[]{:S(2)}) copy-start(bf16[2,128,512]{2,1,0:T(8,128)(2,1)} %get-tuple-element.18) | copy-start | bytes 786436
  194.5 3.4 %copy-start.4 = (f32[2,128,512]{2,1,0:T(8,128)S(1)}, f32[2,128,512]{2,1,0:T(8,128)}, u32[]{:S(2)}) copy-start(f32[2,128,512]{2,1,0:T(8,128)} %get-tuple-element.19) | copy-start | bytes 1572868
  196.0 2.6 %copy-start.7 = (f32[1,1536]{1,0:T(1,128)S(1)}, f32[1,1536]{1,0:T(1,128)}, u32[]{:S(2)}) copy-start(f32[1,1536]{1,0:T(1,128)} %get-tuple-element.20) | copy-start | bytes 18436
  196.0 3.2 %copy-start.6 = (f32[16,512]{1,0:T(8,128)S(1)}, f32[16,512]{1,0:T(8,128)}, u32[]{:S(2)}) copy-start(f32[16,512]{1,0:T(8,128)} %get-tuple-element.24) | copy-start | bytes 98308

commit v3 on v2

--- a/solution.py
+++ b/solution.py
@@ -248,23 +248,24 @@
 
     fill_pick(0)
 
-    pl.semaphore_wait(barrier, z.experts)
-
-    def tell(step, _):
-        pltpu.make_async_remote_copy(
-            src_ref=r.infos.at[0],
-            dst_ref=r.infos.at[step],
-            send_sem=r.info_send,
-            recv_sem=r.info_recv,
-            device_id={"expert": lax.rem(me + step, z.experts)},
-            device_id_type=MESH,
-        ).start()
-        return 0
-
-    lax.fori_loop(1, z.experts, tell, 0)
-    others_told = pl.ds(1, z.experts - 1)
-    owe(SENT, lambda: (r.infos.at[others_told], r.info_send))
-    owe(0, lambda: (r.infos.at[others_told], r.info_recv))
+    def greet_back():
+        pl.semaphore_wait(barrier, z.experts)
+
+        def tell(step, _):
+            pltpu.make_async_remote_copy(
+                src_ref=r.infos.at[0],
+                dst_ref=r.infos.at[step],
+                send_sem=r.info_send,
+                recv_sem=r.info_recv,
+                device_id={"expert": lax.rem(me + step, z.experts)},
+                device_id_type=MESH,
+            ).start()
+            return 0
+
+        lax.fori_loop(1, z.experts, tell, 0)
+        others_told = pl.ds(1, z.experts - 1)
+        owe(SENT, lambda: (r.infos.at[others_told], r.info_send))
+        owe(0, lambda: (r.infos.at[others_told], r.info_recv))
 
     def spread(way, m, half, rows, back):
         packed, landed = (
@@ -361,14 +362,13 @@
         settle(SUMS + 10 * way + m)
         return own + r.sums_in[way, m].astype(F32)
 
-    def know_others():
-        settle(0)
-        fill_pick(1)
+    greet_back()
 
     @dec
     def _():
         dispatch(1, 0, r.cotangent)
-        know_others()
+        settle(0)
+        fill_pick(1)
         dispatch_mirror(1, 0, r.cotangent)
 
     low_lane = jnp.where(iota((1, LANES), 1) < LANES // 2, 1.0, 0.0)
@@ -468,7 +468,8 @@
 
     @enc
     def _():
-        know_others()
+        settle(0)
+        fill_pick(1)
 
     @dec
     def _():
@@ -584,6 +585,7 @@
             expert_forward(m)
             expert_backward(m)
         for m in range(micro):
+            combine(0, m, r.gated[m])
             r.grad_state[m] = r.cotangent[m].astype(F32)
 
     @enc
@@ -679,8 +681,6 @@
             gain_grad += grad_gain
             r.grad_state[m] += grad_state
         r.gain_grads[1:2] = gain_grad
-        for m in range(micro):
-            combine(0, m, r.gated[m])
 
     first_cross = 0
     first_out = first_cross + z.cross_blocks
@@ -991,6 +991,54 @@
     )(*[value for value, _ in inputs.values()])
 
 
+def widen_body(count, *refs):
+    total = (len(refs) - 2) // 4
+    sources, targets, came, made = [refs[i * total : (i + 1) * total] for i in range(4)]
+    come_sem, go_sem = refs[4 * total :]
+    loads = [pltpu.make_async_copy(sources[i], came[i], come_sem.at[i]) for i in range(total)]
+    for copy in loads:
+        copy.start()
+    for i in range(total):
+        loads[i].wait()
+        if i >= count:
+            pltpu.make_async_copy(came[i], targets[i], go_sem.at[i]).start()
+            continue
+        rows, lanes = came[i].shape
+        step_rows = 1 << (min(rows, 128 * 1024 // lanes).bit_length() - 1)
+
+        def step(index, _):
+            at = pl.ds(pl.multiple_of(index * step_rows, step_rows), step_rows)
+            made[i][at] = came[i][at].astype(F32)
+            pltpu.make_async_copy(made[i].at[at], targets[i].at[at], go_sem.at[i]).start()
+            return 0
+
+        lax.fori_loop(0, rows // step_rows, step, 0)
+    for i in range(total):
+        left = made[i] if i < count else came[i]
+        pltpu.make_async_copy(left, targets[i], go_sem.at[i]).wait()
+
+
+def widen(narrow, passed):
+    values = [*narrow, *passed]
+    count = len(narrow)
+    types = [F32] * count + [value.dtype for value in passed]
+    hbm = pl.BlockSpec(memory_space=pltpu.HBM)
+    dma = pltpu.SemaphoreType.DMA((len(values),))
+    blank = pltpu.VMEM((8, LANES), F32)
+    return pl.pallas_call(
+        lambda *refs: widen_body(count, *refs),
+        name="widen",
+        out_shape=[jax.ShapeDtypeStruct(v.shape, t) for v, t in zip(values, types)],
+        in_specs=[hbm] * len(values),
+        out_specs=[hbm] * len(values),
+        scratch_shapes=[pltpu.VMEM(value.shape, value.dtype) for value in values]
+        + [pltpu.VMEM(value.shape, F32) for value in narrow]
+        + [blank] * len(passed)
+        + [dma, dma],
+        compiler_params=pltpu.CompilerParams(vmem_limit_bytes=62 * 1024 * 1024),
+    )(*values)
+
+
 def shards(
     inputs,
     cotangent,
@@ -1024,8 +1072,10 @@
         w_up=w_up[0, 0],
         w_down=w_down[0, 0],
     )
-    out, inputs_grad, gains_grad, router_grad, *grads = run_kernel(z, arrays)
-    qkv_grad, out_grad, cross_grad, up_grad, down_grad = [grad.astype(F32) for grad in grads]
+    *passed, qkv_grad, out_grad, cross_grad, up_grad, down_grad = run_kernel(z, arrays)
+    narrow = (up_grad, down_grad, qkv_grad, cross_grad, out_grad)
+    up_grad, down_grad, qkv_grad, cross_grad, out_grad, *passed = widen(narrow, passed)
+    out, inputs_grad, gains_grad, router_grad = passed
     return (
         out[None],
         inputs_grad[None],

time: 200 us -> 192 us (0.960)
  other arithmetic: 11.6 us -> 0 us
  Pallas kernels: 184 us -> 191 us
  local copies, waits for them, and re-layouts: 2.73 us -> 0 us
    broadcast_in_dim x5 -> x0, other arithmetic: 11.6 us -> none  [the longest x1 4.35 us: shards(): down_grad[None, None]]
    pallas_call x0 -> x1, Pallas kernels: none -> 7.53 us  [widen(): pl.pallas_call(lambda *refs: widen_body(count, *refs), name='widen', out_...]
    unnamed x20 -> x0, local copies, waits for them, and re-layouts: 2.73 us -> none
where the time goes in v3:
time: 192 us
  Pallas kernels  191 us (99%)
    pallas_call x1, Pallas kernels, run_kernel(): pl.pallas_call(body, name='layer_step', out_shape=[jax.ShapeDtypeStruct(s...  183 us
    pallas_call x1, Pallas kernels, widen(): pl.pallas_call(lambda *refs: widen_body(count, *refs), name='widen', out_...  7.53 us

profile of v3, /device:TPU:0, one launch (start us, length us, event | category | flops | bytes accessed | tf_op | source)
XLA Modules:
  0.0 192.3 jit_solution(3149117830374697381)
XLA Ops:
  1.3 183.3 %layer_step.1 = (bf16[2,128,512]{2,1,0:T(8,128)(2,1)}, f32[2,128,512]{2,1,0:T(8,128)}, f32[1,1536]{1,0:T(1,128)}, f32[16,512]{1,0:T(8,128)}, bf16[512,1536]{1,0:...) custom-call(s32[2,128]{1,0:T(2,128)} %bitcast.36, ...), custom_call_target="tpu_custom_call" | custom-call | tf_op jit(solution)/shard_map/layer_step/pallas_call | solution.py:981
  184.6 7.5 %widen.1 = (f32[512,2048]{1,0:T(8,128)}, f32[2048,512]{1,0:T(8,128)}, f32[512,1536]{1,0:T(8,128)}, f32[512,1024]{1,0:T(8,128)}, f32[512,512]{1,0:T(8,128)}, /*in...) custom-call(bf16[512,2048]{1,0:T(8,128)(2,1)} %get-tuple-element.27.refs_0_, ...), custom_call_target="tpu_custom_call" | custom-call | tf_op jit(solution)/shard_map/widen/pallas_call | solution.py:1028
